TPU v7x, 32 devices: a whole 2x2x4 slice. The times are simulated.
32 devices in a mesh: seg: 2 (over x), seq: 16 (over z, y, core).
Axes of the slice: x: 2, y: 2, z: 4, core: 2. Of those that a mesh axis runs over, the one named last changes fastest.
Arguments:
- tokens: bfloat16 [2, 2, 8192, 512], P(None, 'seg', 'seq'), may hold values from -6 to 6
- lengths: int32 [2, 2, 96], replicated, may hold values from 0 to 512, as said below
- qkv_weight: bfloat16 [512, 1536], replicated, may hold values from -0.25 to 0.25
- query_bias: bfloat16 [512], replicated, may hold values from -3 to 3
- value_bias: bfloat16 [512], replicated, may hold values from -3 to 3
- out_weight: bfloat16 [512, 512], replicated, may hold values from -1 to 1
- out_bias: bfloat16 [512], replicated, may hold values from -3 to 3
- attn_gain: bfloat16 [512], replicated, may hold values from 0.5 to 1.5
- attn_shift: bfloat16 [512], replicated, may hold values from -3 to 3
- up_weight: bfloat16 [512, 2048], replicated, may hold values from -0.25 to 0.25
- up_bias: bfloat16 [2048], replicated, may hold values from -3 to 3
- down_weight: bfloat16 [2048, 512], replicated, may hold values from -0.125 to 0.125
- down_bias: bfloat16 [512], replicated, may hold values from -3 to 3
- ffn_gain: bfloat16 [512], replicated, may hold values from 0.5 to 1.5
- ffn_shift: bfloat16 [512], replicated, may hold values from -3 to 3
- cotangent: bfloat16 [2, 2, 8192, 512], P(None, 'seg', 'seq'), may hold values from -6 to 6
Outputs:
- output: bfloat16 [2, 2, 8192, 512], P(None, 'seg', 'seq')
- tokens_grad: float32 [2, 2, 8192, 512], P(None, 'seg', 'seq')
- qkv_weight_grad: float32 [512, 1536], replicated
- query_bias_grad: float32 [512], replicated
- value_bias_grad: float32 [512], replicated
- out_weight_grad: float32 [512, 512], replicated
- out_bias_grad: float32 [512], replicated
- attn_gain_grad: float32 [512], replicated
- attn_shift_grad: float32 [512], replicated
- up_weight_grad: float32 [512, 2048], replicated
- up_bias_grad: float32 [2048], replicated
- down_weight_grad: float32 [2048, 512], replicated
- down_bias_grad: float32 [512], replicated
- ffn_gain_grad: float32 [512], replicated
- ffn_shift_grad: float32 [512], replicated
Inputs may be any that keep to these rules, and one draw needn't show every extreme that they name: `lengths`: A pair spans max of its two counts in slots; spans lie end to end from the first slot in pair order, the same in both segments; no span exceeds 512 and one span of every micro-batch is exactly 512; the shorter count of a pair is at least min(span, 10); the last spans may be cut or empty at the segment's end.
All inputs are finite; a program needn't handle non-finite values.
Results may differ from a plain program's by a relative error of at most 0.014.
Values may be sent and summed in bfloat16 or wider, within the bound.
No kernel may reach another device: no remote copies, remote signals or barrier semaphores. Data moves between devices by JAX's collectives and lax.ppermute only.
A program may use at most 384 MiB of HBM per device.

v0:
```python
import math

import jax
import jax.numpy as jnp
from jax import lax
from jax.sharding import PartitionSpec as P

HEADS = 8
HEAD_DIM = 64
LONGEST = 512


NEG_BIG = -1e30
FLOOR_MAX = -10000.0
EPS = 1e-12


def swapped(value, axis, stride):
    mask = 2**stride
    pairs = [(source, source ^ mask) for source in range(lax.axis_size(axis))]
    return lax.ppermute(value, axis, pairs)


def padded_2(cells, sides, width):
    for axis, dim in sides:
        count = lax.axis_size(axis)
        ends = count - 1
        head = lax.slice_in_dim(cells, 0, width, axis=dim)
        tail = lax.slice_in_dim(cells, cells.shape[dim] - width, cells.shape[dim], axis=dim)
        cells = jnp.concatenate(
            [
                lax.ppermute(tail, axis, [(i, (i + 1) % count) for i in range(ends)]),
                cells,
                lax.ppermute(head, axis, [((i + 1) % count, i) for i in range(ends)]),
            ],
            axis=dim,
        )
    return cells


def passed_along(value, axis, by):
    size = lax.axis_size(axis)
    pairs = [(i, i + by) for i in range(size) if 0 <= i + by < size]
    return lax.ppermute(value, axis, pairs)


def layer_norm(hidden, gain_vec, shift_vec):
    mean_val = jnp.mean(hidden, axis=-1, keepdims=True)
    centred = hidden - mean_val
    var_val = jnp.mean(centred * centred, axis=-1, keepdims=True)
    return centred * lax.rsqrt(var_val + EPS) * gain_vec + shift_vec


def gelu_exact(values):
    return jax.nn.gelu(values, approximate=False)


def table_lookup(index_vec, table):
    labels = jnp.arange(table.shape[0], dtype=jnp.int32)
    return jnp.sum(jnp.where(labels[None, :] == index_vec[:, None], table[None, :], 0), axis=1)


def pair_lookup(positions, lens_pair):
    pair_spans = jnp.maximum(lens_pair[0], lens_pair[1])
    pair_ends = jnp.cumsum(pair_spans)
    pair_starts = pair_ends - pair_spans
    pair_total = pair_spans.shape[0]
    counted = jnp.sum((pair_ends[None, :] <= positions[:, None]).astype(jnp.int32), axis=1)
    safe_idx = jnp.minimum(counted, pair_total - 1)
    start_here = table_lookup(safe_idx, pair_starts)
    inside = (counted < pair_total) & (positions >= start_here)
    offset = positions - start_here
    valid_first = inside & (offset < table_lookup(safe_idx, lens_pair[0]))
    valid_second = inside & (offset < table_lookup(safe_idx, lens_pair[1]))
    pair_id = jnp.where(inside, counted, -1)
    return (pair_id, valid_first, valid_second)


def outer_sum(left, right):
    return lax.dot_general(
        left, right, (((0,), (0,)), ((), ())), preferred_element_type=jnp.float32
    )


def back_product(left, right):
    return lax.dot_general(
        left, right, (((1,), (1,)), ((), ())), preferred_element_type=jnp.float32
    )


def head_major(rows):
    return rows.reshape(rows.shape[0], HEADS, HEAD_DIM).transpose(1, 0, 2)


def row_major(heads):
    return heads.transpose(1, 0, 2).reshape(heads.shape[1], HEADS * HEAD_DIM)


def batched(left, right, left_dim, right_dim):
    return lax.dot_general(
        left, right, (((left_dim,), (right_dim,)), ((0,), (0,))), preferred_element_type=jnp.float32
    )


def masked_scores(query_heads, key_heads, allowed, score_scale):
    raw = batched(query_heads, key_heads, 2, 2)
    return jnp.where(allowed[None], raw * score_scale, NEG_BIG)


def per_device(
    tokens,
    lengths,
    qkv_weight,
    query_bias,
    value_bias,
    out_weight,
    out_bias,
    attn_gain,
    attn_shift,
    up_weight,
    up_bias,
    down_weight,
    down_bias,
    ffn_gain,
    ffn_shift,
    cotangent,
):
    seg_index = lax.axis_index("seg")
    seq_index = lax.axis_index("seq")
    first_seg = seg_index == 0
    model_width = tokens.shape[-1]
    tok_rows = tokens.shape[2]
    margin = LONGEST
    extent = tok_rows + 2 * margin
    key_rows = math.gcd(extent, 512)
    block_count = extent // key_rows
    score_scale = 1.0 / math.sqrt(HEAD_DIM)
    weight_list = (
        qkv_weight,
        query_bias,
        value_bias,
        out_weight,
        out_bias,
        attn_gain,
        attn_shift,
        up_weight,
        up_bias,
        down_weight,
        down_bias,
        ffn_gain,
        ffn_shift,
    )
    grad_sums = [jnp.zeros(item.shape, jnp.float32) for item in weight_list]
    results = []
    input_grads = []
    for micro_idx in range(tokens.shape[0]):
        inputs = tokens[micro_idx, 0]
        lens_pair = lengths[micro_idx]
        key_pos = seq_index * tok_rows - margin + jnp.arange(extent, dtype=jnp.int32)
        key_pair, valid_first, valid_second = pair_lookup(key_pos, lens_pair)
        query_pair = key_pair[margin : margin + tok_rows]
        same_pair = query_pair[:, None] == key_pair[None, :]
        own_mask = same_pair & jnp.where(first_seg, valid_first, valid_second)[None, :]
        other_mask = same_pair & jnp.where(first_seg, valid_second, valid_first)[None, :]
        lin_qkv = jnp.dot(inputs, qkv_weight, preferred_element_type=jnp.float32)
        query = (lin_qkv[:, :model_width] + query_bias).astype(jnp.bfloat16)
        key_part = lin_qkv[:, model_width : 2 * model_width].astype(jnp.bfloat16)
        value_part = (lin_qkv[:, 2 * model_width :] + value_bias).astype(jnp.bfloat16)
        pair_kv = jnp.concatenate([key_part, value_part], axis=1)
        partner_kv = swapped(pair_kv, "seg", 0)
        joined = padded_2(jnp.concatenate([pair_kv, partner_kv], axis=1), (("seq", 0),), margin)
        own_ext = joined[:, : 2 * model_width]
        other_ext = joined[:, 2 * model_width :]
        query_heads = head_major(query)
        blocks = []
        for ext_rows, mask_rows in ((own_ext, own_mask), (other_ext, other_mask)):
            key_all = head_major(ext_rows[:, :model_width])
            value_all = head_major(ext_rows[:, model_width:])
            for block_idx in range(block_count):
                lower = block_idx * key_rows
                upper = lower + key_rows
                blocks.append(
                    (key_all[:, lower:upper], value_all[:, lower:upper], mask_rows[:, lower:upper])
                )
        row_max = jnp.full((HEADS, tok_rows), FLOOR_MAX, jnp.float32)
        row_total = jnp.zeros((HEADS, tok_rows), jnp.float32)
        for key_heads, value_heads, allowed in blocks:
            scores = masked_scores(query_heads, key_heads, allowed, score_scale)
            new_max = jnp.maximum(row_max, jnp.max(scores, axis=-1))
            row_total = row_total * jnp.exp(row_max - new_max) + jnp.sum(
                jnp.exp(scores - new_max[:, :, None]), axis=-1
            )
            row_max = new_max
        denom = jnp.maximum(row_total, 1.0)
        context = jnp.zeros((HEADS, tok_rows, HEAD_DIM), jnp.float32)
        residue = jnp.zeros((HEADS, tok_rows, HEAD_DIM), jnp.float32)
        for key_heads, value_heads, allowed in blocks:
            probs = (
                jnp.exp(
                    masked_scores(query_heads, key_heads, allowed, score_scale)
                    - row_max[:, :, None]
                )
                / denom[:, :, None]
            )
            probs_high = probs.astype(jnp.bfloat16)
            probs_low = (probs - probs_high.astype(jnp.float32)).astype(jnp.bfloat16)
            context = context + batched(probs_high, value_heads, 2, 1)
            residue = residue + batched(probs_low, value_heads, 2, 1)
        context_r = row_major(context).astype(jnp.bfloat16)
        h_first = (
            inputs.astype(jnp.float32)
            + jnp.dot(context_r, out_weight, preferred_element_type=jnp.float32)
            + out_bias
        )
        normed, norm_first_back = jax.vjp(
            layer_norm, h_first, attn_gain.astype(jnp.float32), attn_shift.astype(jnp.float32)
        )
        normed_r = normed.astype(jnp.bfloat16)
        pre_act = jnp.dot(normed_r, up_weight, preferred_element_type=jnp.float32) + up_bias
        act_val, act_back = jax.vjp(gelu_exact, pre_act)
        act_r = act_val.astype(jnp.bfloat16)
        h_second = (
            normed + jnp.dot(act_r, down_weight, preferred_element_type=jnp.float32) + down_bias
        )
        result, norm_second_back = jax.vjp(
            layer_norm, h_second, ffn_gain.astype(jnp.float32), ffn_shift.astype(jnp.float32)
        )
        results.append(result.astype(jnp.bfloat16))
        d_h_second, d_gain_second, d_shift_second = norm_second_back(
            cotangent[micro_idx, 0].astype(jnp.float32)
        )
        d_down_r = d_h_second.astype(jnp.bfloat16)
        d_act = back_product(d_down_r, down_weight)
        d_pre_r = act_back(d_act)[0].astype(jnp.bfloat16)
        d_normed = d_h_second + back_product(d_pre_r, up_weight)
        d_h_first, d_gain_first, d_shift_first = norm_first_back(d_normed)
        d_attn_r = d_h_first.astype(jnp.bfloat16)
        d_context = head_major(back_product(d_attn_r, out_weight).astype(jnp.bfloat16))
        delta = jnp.sum(d_context.astype(jnp.float32) * (context + residue), axis=-1)
        d_query = jnp.zeros((HEADS, tok_rows, HEAD_DIM), jnp.float32)
        key_grads = []
        for key_heads, value_heads, allowed in blocks:
            probs = (
                jnp.exp(
                    masked_scores(query_heads, key_heads, allowed, score_scale)
                    - row_max[:, :, None]
                )
                / denom[:, :, None]
            )
            probs_high = probs.astype(jnp.bfloat16)
            d_probs = batched(d_context, value_heads, 2, 2)
            d_scores = (probs * (d_probs - delta[:, :, None])).astype(jnp.bfloat16)
            d_query = d_query + batched(d_scores, key_heads, 2, 1) * score_scale
            d_key = batched(d_scores, query_heads, 1, 1) * score_scale
            d_value = batched(probs_high, d_context, 1, 1)
            key_grads.append(jnp.concatenate([row_major(d_key), row_major(d_value)], axis=1))
        own_grad = jnp.concatenate(key_grads[:block_count], axis=0)
        other_grad = jnp.concatenate(key_grads[block_count:], axis=0)
        returned = swapped(other_grad.astype(jnp.bfloat16), "seg", 0).astype(other_grad.dtype)
        ext_grad = own_grad + returned
        from_above = passed_along(ext_grad[:margin].astype(jnp.bfloat16), "seq", -1).astype(
            jnp.float32
        )
        from_below = passed_along(
            ext_grad[margin + tok_rows :].astype(jnp.bfloat16), "seq", 1
        ).astype(jnp.float32)
        kv_grad = ext_grad[margin : margin + tok_rows] + from_above + from_below
        d_query_flat = row_major(d_query)
        d_lin = jnp.concatenate([d_query_flat, kv_grad], axis=1).astype(jnp.bfloat16)
        step_grads = (
            outer_sum(inputs, d_lin),
            jnp.sum(d_query_flat, axis=0),
            jnp.sum(kv_grad[:, model_width:], axis=0),
            outer_sum(context_r, d_attn_r),
            jnp.sum(d_h_first, axis=0),
            d_gain_first,
            d_shift_first,
            outer_sum(normed_r, d_pre_r),
            jnp.sum(d_pre_r.astype(jnp.float32), axis=0),
            outer_sum(act_r, d_down_r),
            jnp.sum(d_h_second, axis=0),
            d_gain_second,
            d_shift_second,
        )
        grad_sums = [prior + update for prior, update in zip(grad_sums, step_grads)]
        input_grads.append(d_h_first + back_product(d_lin, qkv_weight))
    flat_grads = jnp.concatenate([item.reshape(-1) for item in grad_sums])
    device_count = lax.axis_size("seg") * lax.axis_size("seq")
    total_len = flat_grads.shape[0]
    column_count = -(-total_len // device_count)
    column_count = -(-column_count // 128) * 128
    padded = jnp.pad(flat_grads, (0, column_count * device_count - total_len))
    strided = padded.reshape(column_count, device_count).T
    grad_share = lax.psum_scatter(strided, ("seg", "seq"), scatter_dimension=0, tiled=True)
    summed_all = lax.all_gather(
        grad_share.astype(jnp.bfloat16), ("seg", "seq"), axis=0, tiled=True
    ).astype(grad_share.dtype)
    summed = summed_all.T.reshape(-1)
    outputs_list = []
    offset = 0
    for item in grad_sums:
        item_size = item.size
        outputs_list.append(summed[offset : offset + item_size].reshape(item.shape))
        offset += item_size
    return (
        jnp.stack(results)[:, None],
        jnp.stack(input_grads)[:, None],
        outputs_list[0],
        outputs_list[1],
        outputs_list[2],
        outputs_list[3],
        outputs_list[4],
        outputs_list[5],
        outputs_list[6],
        outputs_list[7],
        outputs_list[8],
        outputs_list[9],
        outputs_list[10],
        outputs_list[11],
        outputs_list[12],
    )


def solution(mesh):
    in_specs = (
        P(None, "seg", "seq", None),
        P(),
        P(),
        P(),
        P(),
        P(),
        P(),
        P(),
        P(),
        P(),
        P(),
        P(),
        P(),
        P(),
        P(),
        P(None, "seg", "seq", None),
    )
    out_specs = (
        P(None, "seg", "seq", None),
        P(None, "seg", "seq", None),
        P(),
        P(),
        P(),
        P(),
        P(),
        P(),
        P(),
        P(),
        P(),
        P(),
        P(),
        P(),
        P(),
    )
    return jax.shard_map(
        per_device, mesh=mesh, in_specs=in_specs, out_specs=out_specs, check_vma=False
    )
```

profile of v0, /device:TPU:0, one launch (start us, length us, event | category | flops | bytes accessed | tf_op | source)
XLA Modules:
  0.0 1844.2 jit_solution(5105345393450320904)
XLA Ops:
  37.6 5.0 collective-permute-done.3
  54.3 10.0 collective-permute-done
  68.4 4.4 collective-permute-start.1
  90.3 4.8 fusion.13
  96.7 5.2 fusion.12
  101.9 4.8 fusion.11
  111.6 5.3 exponential_reduce_fusion.1
  118.7 5.1 exponential_reduce_fusion.3
  138.2 6.4 convolution_add_fusion.13
  144.6 4.9 convolution_add_fusion.12
  154.6 4.6 fusion.25
  176.8 5.3 fusion.7
  182.1 4.7 fusion.6
  188.4 5.3 fusion.5
  198.4 5.7 exponential_reduce_fusion.5
  204.1 5.3 exponential_reduce_fusion.6
  227.1 6.4 convolution_add_fusion.18
  233.6 4.9 convolution_add_fusion.17
  244.1 20.9 %multiply_convert_fusion.13 = (bf16[512,2048]{1,0:T(8,128)(2,1)S(1)}, f32[512,2048]{1,0:T(8,128)S(1)}, bf16[512,2048]{1,0:T(8,128)(2,1)S(1)}, f32[512,2048]{1,0:T(8,128)S(1)}, f32[512,2048]{1,0:T(8,128)S(1)}) fusion(f32[2048]{0:T(1024)S(1)} %copy-done.184, f32[512,2048]{1,0:T(8,128)S(1)} %fusion.247, bf16[512,2048]{1,0:T(8,128)(2,1)S(1)} %copy-done, ...), kind=kOutput, calls=%fused_computation.116 | convolution fusion | flops 1213464576 | bytes 24133632 | tf_op jit(solution)/shard_map/dot_general | solution.py:219
  293.1 5.2 fusion.61
  298.3 5.2 fusion.60
  311.9 4.4 multiply_convert_fusion
  316.3 4.7 multiply_convert_fusion.1
  324.2 5.7 multiply_convert_fusion.2
  333.1 4.4 multiply_convert_fusion.3
  340.8 4.5 multiply_convert_fusion.4
  348.7 4.7 multiply_convert_fusion.5
  371.6 5.3 fusion.65
  379.7 5.1 fusion.63
  390.9 6.7 multiply_convert_fusion.7
  400.9 4.6 multiply_convert_fusion.8
  405.5 6.1 fusion.228
  411.6 6.6 multiply_convert_fusion.9
  418.2 4.4 multiply_convert_fusion.10
  444.9 15.7 maximum_maximum_fusion.1
  462.3 4.5 convolution_multiply_fusion.3
  466.9 4.6 convolution_multiply_fusion.4
  487.5 19.0 %maximum_maximum_fusion = bf16[1536,1024]{0,1:T(8,128)(2,1)} fusion(bf16[512,512]{0,1:T(8,128)(2,1)S(1)} %bitcast.493, bf16[512,512]{0,1:T(8,128)(2,1)S(1)} %bitcast.429, bf16[512,512]{0,1:T(8,128)(2,1)S(1)} %bitcast.494, bf16[512,512]{0,1:T(8,128)(2,1)S(1)} %bitcast.430, bf16[512,512]{0,1:T(8,128)(2,1)} %bitcast.496, bf16[512,512]{0,1:T(8,128)(2,1)S(1)} %bitcast.431), kind=kLoop, calls=%fused_computation.137 | loop fusion | flops 18874368 | bytes 6291456 | tf_op jit(solution)/shard_map/concatenate | solution.py:258
  509.5 4.5 convolution_multiply_fusion.10
  528.6 4.4 fusion.232
  539.7 38.3 %collective-permute-done.6 = bf16[1536,1024]{0,1:T(8,128)(2,1)} collective-permute-done((bf16[1536,1024]{0,1:T(8,128)(2,1)}, bf16[1536,1024]{0,1:T(8,128)(2,1)}, u32[]{:S(2)}, u32[]{:S(2)}) %collective-permute-start.6) | collective-permute-done | bytes 3145760 | tf_op jit(solution)/shard_map/ppermute | solution.py:21
  578.0 8.6 fusion.261
  589.6 33.1 %collective-permute-start.8 = (bf16[512,1024]{0,1:T(8,128)(2,1)}, bf16[512,1024]{0,1:T(8,128)(2,1)}, u32[]{:S(2)}, u32[]{:S(2)}) collective-permute-start(bf16[512,1024]{0,1:T(8,128)(2,1)} %get-tuple-element.163), channel_id=1, source_target_pairs={{0,1},{1,2},{2,3},{3,4},{4,5},{5,6},{6,7},{7,8},{8,9},{9,10},{10,1... | collective-permute-start | bytes 3145736 | tf_op jit(solution)/shard_map/ppermute | solution.py:44
  624.0 8.6 fusion.266
  635.7 6.2 collective-permute-start.11
  646.3 5.1 copy.620
  654.8 4.1 fusion.259
  671.2 4.4 reshape.781
  687.5 36.6 %dynamic-update-slice.7 = f32[3151872]{0:T(1024)} dynamic-update-slice(f32[3151872]{0:T(1024)} %constant_dynamic-update-slice_fusion.3, f32[1048576]{0:T(1024)} %bitcast.392, s32[]{} %constant.139) | dynamic-update-slice | bytes 8388612
  725.5 36.5 %dynamic-update-slice.9 = f32[3151872]{0:T(1024)} dynamic-update-slice(f32[3151872]{0:T(1024)} %add_dynamic-update-slice_fusion, f32[1048576]{0:T(1024)} %bitcast.391, s32[]{} %constant.141) | dynamic-update-slice | bytes 8388612
  765.8 9.4 pad.4
  775.1 30.4 %reshape.785 = f32[98560,32]{1,0:T(8,128)} reshape(f32[3153920]{0:T(1024)} %pad.4) | data formatting | bytes 25231360 | tf_op jit(solution)/shard_map/reshape | solution.py:293
  805.5 811.9 %all-reduce.3 = bf16[32,98560]{0,1:T(8,128)(2,1)} all-reduce(f32[32,98560]{0,1:T(8,128)} %bitcast.321), channel_id=2, replica_groups=mesh['seg'=2,'seq'=16] {'seg','seq'}, use_global_device_ids=true, to_apply=%region_70.71.clone | all-reduce | flops 3153920 | bytes 18923520
  1617.4 18.7 %fusion = bf16[98560]{0:T(1024)(128)(2,1)S(1)} fusion(bf16[32,98560]{0,1:T(8,128)(2,1)} %all-reduce.3, u32[]{:T(128)S(6)} %add.612), kind=kLoop, calls=%fused_computation.1 | loop fusion | bytes 394244 | tf_op jit(solution)/shard_map/convert_element_type | solution.py:296
  1645.9 85.5 %all-gather.3.cloned.1.call-done = bf16[32,1,98560]{2,1,0:T(2,128)(2,1)} async-done(((bf16[1,1,98560]{2,1,0:T(2,128)(2,1)}), bf16[32,1,98560]{2,1,0:T(2,128)(2,1)}) %all-gather.3.cloned.1.call-update) | async-done | bytes 6307856 | tf_op jit(solution)/shard_map/all_gather | solution.py:295
  1731.4 10.0 copy.623
  1747.7 9.1 fusion.276
  1757.7 8.4 copy.521
  1766.1 10.0 reshape.786
  1780.2 4.4 reshape.787
  1786.8 10.4 copy.528
  1797.2 13.4 reshape.788
  1811.3 10.5 copy.530
  1821.8 12.9 reshape.789
  (760 shorter events, 350.7 us)
Async XLA Ops:
  7.2 235.5 %copy-start = (bf16[512,2048]{1,0:T(8,128)(2,1)S(1)}, bf16[512,2048]{1,0:T(8,128)(2,1)}, u32[]{:S(2)}) copy-start(bf16[512,2048]{1,0:T(8,128)(2,1)} %param.25) | copy-start | bytes 6291460
  7.2 1724.2 %all-gather.3.cloned.1.call-start = ((), (), s32[]{:S(2)}) async-start(), calls=%async_computation | async-start | bytes 13009920 | tf_op jit(solution)/shard_map/all_gather | solution.py:295
  14.3 11.1 copy-start.196
  14.3 11.7 copy-start.188
  14.3 12.3 copy-start.197
  15.4 27.2 %collective-permute-start.3 = (bf16[512,1024]{1,0:T(8,128)(2,1)}, bf16[512,1024]{1,0:T(8,128)(2,1)}, u32[]{:S(2)}, u32[]{:S(2)}) collective-permute-start(bf16[512,1024]{1,0:T(8,128)(2,1)} %pad_maximum_fusion.7), channel_id=1, source_target_pairs={{0,16},{16,0},{1,17},{17,1},{2,18},{18,2},{3,19},{19,3},{4,20},{20... | collective-permute-start | bytes 3145736 | tf_op jit(solution)/shard_map/ppermute | solution.py:21
  18.4 11.7 copy-start.198
  18.4 12.3 copy-start.199
  19.5 15.3 copy-start.200
  19.5 15.9 copy-start.201
  19.5 44.7 %collective-permute-start = (bf16[512,1024]{1,0:T(8,128)(2,1)}, bf16[512,1024]{1,0:T(8,128)(2,1)}, u32[]{:S(2)}, u32[]{:S(2)}) collective-permute-start(bf16[512,1024]{1,0:T(8,128)(2,1)} %pad_maximum_fusion.6), channel_id=1, source_target_pairs={{0,16},{16,0},{1,17},{17,1},{2,18},{18,2},{3,19},{19,3},{4,20},{20... | collective-permute-start | bytes 3145736 | tf_op jit(solution)/shard_map/ppermute | solution.py:21
  27.9 74.0 %copy-start.4 = (bf16[512,512]{0,1:T(8,128)(2,1)}, bf16[512,512]{0,1:T(8,128)(2,1)S(1)}, u32[]{:S(2)}) copy-start(bf16[512,512]{0,1:T(8,128)(2,1)S(1)} %copy.443) | copy-start | bytes 1572868
  32.6 161.1 %copy-start.2 = (bf16[512,512]{0,1:T(8,128)(2,1)}, bf16[512,512]{0,1:T(8,128)(2,1)S(1)}, u32[]{:S(2)}) copy-start(bf16[512,512]{0,1:T(8,128)(2,1)S(1)} %copy.430) | copy-start | bytes 1572868
  37.6 26.7 %copy-start.51 = (bf16[512,512]{1,0:T(8,128)(2,1)S(1)}, bf16[512,512]{1,0:T(8,128)(2,1)}, u32[]{:S(2)}) copy-start(bf16[512,512]{1,0:T(8,128)(2,1)} %copy-done.50) | copy-start | bytes 1572868
  37.6 26.7 %copy-start.56 = (bf16[512,512]{1,0:T(8,128)(2,1)S(1)}, bf16[512,512]{1,0:T(8,128)(2,1)}, u32[]{:S(2)}) copy-start(bf16[512,512]{1,0:T(8,128)(2,1)} %copy-done.55) | copy-start | bytes 1572868
  44.3 28.4 %copy-start.54 = (bf16[512,512]{1,0:T(8,128)(2,1)S(1)}, bf16[512,512]{1,0:T(8,128)(2,1)}, u32[]{:S(2)}) copy-start(bf16[512,512]{1,0:T(8,128)(2,1)} %copy-done.53) | copy-start | bytes 1572868
  44.4 28.4 %copy-start.59 = (bf16[512,512]{1,0:T(8,128)(2,1)S(1)}, bf16[512,512]{1,0:T(8,128)(2,1)}, u32[]{:S(2)}) copy-start(bf16[512,512]{1,0:T(8,128)(2,1)} %copy-done.58) | copy-start | bytes 1572868
  44.4 28.4 %collective-permute-start.5 = (bf16[512,2048]{1,0:T(8,128)(2,1)S(1)}, bf16[512,2048]{1,0:T(8,128)(2,1)S(1)}, u32[]{:S(2)}, u32[]{:S(2)}) collective-permute-start(bf16[512,2048]{1,0:T(8,128)(2,1)S(1)} %pad_maximum_fusion.3), channel_id=1, source_target_pairs={{1,0},{2,1},{3,2},{4,3},{5,4},{6,5},{7,6},{8,7},{9,8},{10,9},{11,1... | collective-permute-start | bytes 6291464 | tf_op jit(solution)/shard_map/ppermute | solution.py:34
  45.8 27.0 %collective-permute-start.4 = (bf16[512,2048]{1,0:T(8,128)(2,1)S(1)}, bf16[512,2048]{1,0:T(8,128)(2,1)S(1)}, u32[]{:S(2)}, u32[]{:S(2)}) collective-permute-start(bf16[512,2048]{1,0:T(8,128)(2,1)S(1)} %pad_maximum_fusion.3), channel_id=1, source_target_pairs={{0,1},{1,2},{2,3},{3,4},{4,5},{5,6},{6,7},{7,8},{8,9},{9,10},{10,1... | collective-permute-start | bytes 6291464 | tf_op jit(solution)/shard_map/ppermute | solution.py:32
  53.4 161.3 %copy-start.74 = (pred[512,512]{0,1:T(8,128)(4,1)}, pred[512,512]{0,1:T(8,128)(4,1)S(1)}, u32[]{:S(2)}) copy-start(pred[512,512]{0,1:T(8,128)(4,1)S(1)} %get-tuple-element.180) | copy-start | bytes 786436
  67.1 92.2 %collective-permute-start.2 = (bf16[512,2048]{1,0:T(8,128)(2,1)}, bf16[512,2048]{1,0:T(8,128)(2,1)}, u32[]{:S(2)}, u32[]{:S(2)}) collective-permute-start(bf16[512,2048]{1,0:T(8,128)(2,1)} %pad_maximum_fusion.2), channel_id=1, source_target_pairs={{1,0},{2,1},{3,2},{4,3},{5,4},{6,5},{7,6},{8,7},{9,8},{10,9},{11,1... | collective-permute-start | bytes 6291464 | tf_op jit(solution)/shard_map/ppermute | solution.py:34
  68.4 90.9 %collective-permute-start.1 = (bf16[512,2048]{1,0:T(8,128)(2,1)}, bf16[512,2048]{1,0:T(8,128)(2,1)}, u32[]{:S(2)}, u32[]{:S(2)}) collective-permute-start(bf16[512,2048]{1,0:T(8,128)(2,1)} %pad_maximum_fusion.2), channel_id=1, source_target_pairs={{0,1},{1,2},{2,3},{3,4},{4,5},{5,6},{6,7},{7,8},{8,9},{9,10},{10,1... | collective-permute-start | bytes 6291464 | tf_op jit(solution)/shard_map/ppermute | solution.py:32
  88.7 18.0 copy-start.10
  90.3 19.2 %copy-start.11 = (f32[8,512,512]{1,2,0:T(8,128)}, f32[8,512,512]{1,2,0:T(8,128)S(1)}, u32[]{:S(2)}) copy-start(f32[8,512,512]{1,2,0:T(8,128)S(1)} %get-tuple-element.239) | copy-start | bytes 25165828
  96.6 29.0 %copy-start.9 = (f32[8,512,512]{1,2,0:T(8,128)}, f32[8,512,512]{1,2,0:T(8,128)S(1)}, u32[]{:S(2)}) copy-start(f32[8,512,512]{1,2,0:T(8,128)S(1)} %get-tuple-element.247) | copy-start | bytes 25165828
  106.7 47.8 %copy-start.155 = (f32[8,512]{1,0:T(8,128)}, f32[8,512]{1,0:T(8,128)S(1)}, u32[]{:S(2)}) copy-start(f32[8,512]{1,0:T(8,128)S(1)} %get-tuple-element.136) | copy-start | bytes 49156
  125.6 28.9 %copy-start.176 = (f32[8,512]{1,0:T(8,128)}, f32[8,512]{1,0:T(8,128)S(1)}, u32[]{:S(2)}) copy-start(f32[8,512]{1,0:T(8,128)S(1)} %add_maximum_fusion) | copy-start | bytes 49156
  138.2 11.3 slice-start.10
  153.4 129.3 %copy-start.151 = (f32[512]{0:T(512)}, f32[512]{0:T(512)S(1)}, u32[]{:S(2)}) copy-start(f32[512]{0:T(512)S(1)} %broadcast_multiply_fusion.1) | copy-start | bytes 6148
  154.6 128.2 %copy-start.157 = (f32[512]{0:T(512)}, f32[512]{0:T(512)S(1)}, u32[]{:S(2)}) copy-start(f32[512]{0:T(512)S(1)} %fusion.192) | copy-start | bytes 6148
  176.8 18.4 copy-start.12
  188.4 26.3 %copy-start.7 = (f32[8,512,512]{1,2,0:T(8,128)}, f32[8,512,512]{1,2,0:T(8,128)S(1)}, u32[]{:S(2)}) copy-start(f32[8,512,512]{1,2,0:T(8,128)S(1)} %get-tuple-element.231) | copy-start | bytes 25165828
  195.2 23.2 %copy-start.8 = (f32[8,512,512]{1,2,0:T(8,128)}, f32[8,512,512]{1,2,0:T(8,128)S(1)}, u32[]{:S(2)}) copy-start(f32[8,512,512]{1,2,0:T(8,128)S(1)} %get-tuple-element.229) | copy-start | bytes 25165828
  195.2 43.2 %copy-start.153 = (f32[8,512]{1,0:T(8,128)}, f32[8,512]{1,0:T(8,128)S(1)}, u32[]{:S(2)}) copy-start(f32[8,512]{1,0:T(8,128)S(1)} %get-tuple-element.126) | copy-start | bytes 49156
  198.3 11.0 slice-start.38
  214.7 23.8 %copy-start.174 = (f32[8,512]{1,0:T(8,128)}, f32[8,512]{1,0:T(8,128)S(1)}, u32[]{:S(2)}) copy-start(f32[8,512]{1,0:T(8,128)S(1)} %add_maximum_fusion.1) | copy-start | bytes 49156
  227.1 11.3 slice-start.26
  242.4 40.4 %copy-start.29 = (f32[512,512]{0,1:T(8,128)}, f32[512,512]{0,1:T(8,128)S(1)}, u32[]{:S(2)}) copy-start(f32[512,512]{0,1:T(8,128)S(1)} %get-tuple-element.235) | copy-start | bytes 3145732
  242.4 40.4 %copy-start.159 = (f32[512]{0:T(512)}, f32[512]{0:T(512)S(1)}, u32[]{:S(2)}) copy-start(f32[512]{0:T(512)S(1)} %broadcast_multiply_fusion.3) | copy-start | bytes 6148
  242.7 40.1 %copy-start.163 = (f32[512]{0:T(512)}, f32[512]{0:T(512)S(1)}, u32[]{:S(2)}) copy-start(f32[512]{0:T(512)S(1)} %fusion.190) | copy-start | bytes 6148
  244.1 21.0 %copy-start.193 = (f32[512]{0:T(512)S(1)}, f32[512]{0:T(512)}, u32[]{:S(2)}) copy-start(f32[512]{0:T(512)} %convert_element_type.348) | copy-start | bytes 6148
  244.1 20.9 %copy-start.202 = (bf16[2048,512]{1,0:T(8,128)(2,1)S(1)}, bf16[2048,512]{1,0:T(8,128)(2,1)}, u32[]{:S(2)}) copy-start(bf16[2048,512]{1,0:T(8,128)(2,1)} %param.27) | copy-start | bytes 6291460
  293.1 10.4 slice-start.16
  345.3 13.6 slice-start
  411.6 11.0 slice-start.2
  460.6 10.8 copy-start.34
  460.6 10.8 copy-start.70
  460.6 163.4 %collective-permute-start.9 = (bf16[1536,1024]{0,1:T(8,128)(2,1)}, bf16[1536,1024]{0,1:T(8,128)(2,1)}, u32[]{:S(2)}, u32[]{:S(2)}) collective-permute-start(bf16[1536,1024]{0,1:T(8,128)(2,1)} %maximum_maximum_fusion.1), channel_id=1, source_target_pairs={{0,16},{16,0},{1,17},{17,1},{2,18},{18,2},{3,19},{19,3},{4,20},{20... | collective-permute-start | bytes 9437192 | tf_op jit(solution)/shard_map/ppermute | solution.py:21
  487.5 19.6 %copy-start.25 = (bf16[8,512,512]{1,2,0:T(8,128)(2,1)S(1)}, bf16[8,512,512]{1,2,0:T(8,128)(2,1)}, u32[]{:S(2)}) copy-start(bf16[8,512,512]{1,2,0:T(8,128)(2,1)} %multiply_convert_fusion.9) | copy-start | bytes 12582916
  506.6 71.4 %collective-permute-start.6 = (bf16[1536,1024]{0,1:T(8,128)(2,1)}, bf16[1536,1024]{0,1:T(8,128)(2,1)}, u32[]{:S(2)}, u32[]{:S(2)}) collective-permute-start(bf16[1536,1024]{0,1:T(8,128)(2,1)} %maximum_maximum_fusion), channel_id=1, source_target_pairs={{0,16},{16,0},{1,17},{17,1},{2,18},{18,2},{3,19},{19,3},{4,20},{20... | collective-permute-start | bytes 9437192 | tf_op jit(solution)/shard_map/ppermute | solution.py:21
  589.6 65.2 %collective-permute-start.8 = (bf16[512,1024]{0,1:T(8,128)(2,1)}, bf16[512,1024]{0,1:T(8,128)(2,1)}, u32[]{:S(2)}, u32[]{:S(2)}) collective-permute-start(bf16[512,1024]{0,1:T(8,128)(2,1)} %get-tuple-element.163), channel_id=1, source_target_pairs={{0,1},{1,2},{2,3},{3,4},{4,5},{5,6},{6,7},{7,8},{8,9},{9,10},{10,1... | collective-permute-start | bytes 3145736 | tf_op jit(solution)/shard_map/ppermute | solution.py:44
  622.7 32.1 %collective-permute-start.7 = (bf16[512,1024]{0,1:T(8,128)(2,1)}, bf16[512,1024]{0,1:T(8,128)(2,1)}, u32[]{:S(2)}, u32[]{:S(2)}) collective-permute-start(bf16[512,1024]{0,1:T(8,128)(2,1)} %get-tuple-element.162), channel_id=1, source_target_pairs={{1,0},{2,1},{3,2},{4,3},{5,4},{6,5},{7,6},{8,7},{9,8},{10,9},{11,1... | collective-permute-start | bytes 3145736 | tf_op jit(solution)/shard_map/ppermute | solution.py:44
  635.7 24.3 %collective-permute-start.11 = (bf16[512,1024]{0,1:T(8,128)(2,1)}, bf16[512,1024]{0,1:T(8,128)(2,1)}, u32[]{:S(2)}, u32[]{:S(2)}) collective-permute-start(bf16[512,1024]{0,1:T(8,128)(2,1)} %get-tuple-element.165), channel_id=1, source_target_pairs={{0,1},{1,2},{2,3},{3,4},{4,5},{5,6},{6,7},{7,8},{8,9},{9,10},{10,1... | collective-permute-start | bytes 3145736 | tf_op jit(solution)/shard_map/ppermute | solution.py:44
  641.9 18.1 collective-permute-start.10
  671.2 11.3 copy-start.68
  675.7 10.5 copy-start.189
  675.7 10.5 copy-start.190
  679.6 44.5 %copy-start.182 = (f32[2048]{0:T(1024)S(1)}, f32[2048]{0:T(1024)}, u32[]{:S(2)}) copy-start(f32[2048]{0:T(1024)} %get-tuple-element.262) | copy-start | bytes 24580
  679.6 44.5 %copy-start.183 = (f32[2048]{0:T(1024)S(1)}, f32[2048]{0:T(1024)}, u32[]{:S(2)}) copy-start(f32[2048]{0:T(1024)} %get-tuple-element.260) | copy-start | bytes 24580
  724.1 39.1 %copy-start.186 = (f32[512]{0:T(512)S(1)}, f32[512]{0:T(512)}, u32[]{:S(2)}) copy-start(f32[512]{0:T(512)} %get-tuple-element.96) | copy-start | bytes 6148
  724.1 39.1 %copy-start.187 = (f32[512]{0:T(512)S(1)}, f32[512]{0:T(512)}, u32[]{:S(2)}) copy-start(f32[512]{0:T(512)} %get-tuple-element.211) | copy-start | bytes 6148
  724.1 40.4 %copy-start.178 = (f32[512]{0:T(512)S(1)}, f32[512]{0:T(512)}, u32[]{:S(2)}) copy-start(f32[512]{0:T(512)} %get-tuple-element.269) | copy-start | bytes 6148
  724.1 40.4 %copy-start.179 = (f32[512]{0:T(512)S(1)}, f32[512]{0:T(512)}, u32[]{:S(2)}) copy-start(f32[512]{0:T(512)} %get-tuple-element.270) | copy-start | bytes 6148
  1811.3 25.6 %copy-start.1 = (bf16[512,2048]{1,0:T(8,128)(2,1)S(1)}, bf16[512,2048]{1,0:T(8,128)(2,1)}, u32[]{:S(2)}) copy-start(bf16[512,2048]{1,0:T(8,128)(2,1)} %param.25) | copy-start | bytes 6291460
  (195 other events, 901.0 us)
Sparse Core Ops, SparseCore 0:
  1637.2 94.1 all-gather.2
where the time goes:
time: 1860 us; the launch traced here: 1840 us
  blocking collectives  812 us (44%)
  matrix products  359 us (19%)
  local copies, waits for them, and re-layouts  319 us (17%)
  other arithmetic  140 us (8%)
  waiting for transfers between devices  139 us (7%)
  starting transfers between devices  57.5 us (3%)
    unnamed x1, blocking collectives  812 us
    dot_general x84, matrix products, batched(): lax.dot_general(left, right, (((left_dim,), (right_dim,)), ((0,), (0,))),...  296 us
    unnamed x508, local copies, waits for them, and re-layouts  116 us
    all_gather x1, waiting for transfers between devices, per_device(): lax.all_gather(grad_share.astype(jnp.bfloat16), ('seg', 'seq'), axis=0, t...  85.5 us
    slice x27, local copies, waits for them, and re-layouts, per_device(): outputs_list.append(summed[offset:offset + item_size].reshape(item.shape))  54.8 us
    ppermute x4, waiting for transfers between devices, swapped(): return lax.ppermute(value, axis, pairs)  53.2 us
    ppermute x4, starting transfers between devices, passed_along(): return lax.ppermute(value, axis, pairs)  42 us
    reshape x4, local copies, waits for them, and re-layouts, per_device(): outputs_list.append(summed[offset:offset + item_size].reshape(item.shape))  40.7 us
  transfers between devices with their start and end apart: 13, of which 4 were waited for; matrix products, arithmetic and copies ran while one was open for 13% of the time, Pallas kernels for 0%

commit v1 on v0

v1 whole, which is shorter than its diff:
```python
import functools
import math

import jax
import jax.numpy as jnp
from jax import lax
from jax.experimental import pallas as pl
from jax.experimental.pallas import tpu as pltpu
from jax.sharding import PartitionSpec as P

HEADS = 8
HEAD_DIM = 64
LONGEST = 512
FLOOR_MAX = -10000.0
MASK_OFF = -1e30
EPS = 1e-12
LANES = 128
SLOT_TILE = 128
DIGIT = 13
DIGITS = 3
BAD_LANE = DIGIT * DIGITS
STAT_LANE = BAD_LANE + 1
GROUP = HEADS // 2
WIDE = GROUP * HEAD_DIM
PAIRED = WIDE // LANES
CHAIN_ROWS = 256
BF = jnp.bfloat16
F32 = jnp.float32
ANY = pl.BlockSpec(memory_space=pl.ANY)
SMEM = pl.BlockSpec(memory_space=pltpu.SMEM)


def whole(shape):
    zeros = (0,) * len(shape)
    return pl.BlockSpec(shape, lambda _: zeros)


def row_block(rows, cols):
    return pl.BlockSpec((rows, cols), lambda i: (i, 0))


def vmem(mega):
    return pltpu.CompilerParams(vmem_limit_bytes=mega * 1024 * 1024)


def cost(giga, mega):
    return pl.CostEstimate(
        flops=int(giga * 10**9), bytes_accessed=int(mega * 10**6), transcendentals=0
    )


def dot_nn(left, right):
    return lax.dot_general(left, right, (((1,), (0,)), ((), ())), preferred_element_type=F32)


def dot_nt(left, right):
    return lax.dot_general(left, right, (((1,), (1,)), ((), ())), preferred_element_type=F32)


def dot_tn(left, right):
    return lax.dot_general(left, right, (((0,), (0,)), ((), ())), preferred_element_type=F32)


def lanes_of(rows):
    return lax.broadcasted_iota(jnp.int32, (rows, LANES), 1)


def in_head(head, rows):
    lane = lanes_of(rows)
    return lane < HEAD_DIM if head % 2 == 0 else lane >= HEAD_DIM


def stat_lane(head):
    return STAT_LANE + 3 * head + (HEAD_DIM if head % 2 == 0 else 0)


def ones_row(head, rows):
    lane = lanes_of(rows)
    first = stat_lane(head)
    return ((lane >= first) & (lane < first + 3)).astype(F32).astype(BF)


def pair_cols(part, head):
    first = part * WIDE + (head // 2) * LANES
    return slice(first, first + LANES)


def both(ref, start, cols):
    return jnp.concatenate(
        [ref[seg, pl.ds(start, SLOT_TILE), cols] for seg in range(2)], axis=0
    )


def three_parts(values):
    high = values.astype(BF).astype(F32)
    rest = values - high
    mid = rest.astype(BF).astype(F32)
    low = (rest - mid).astype(BF).astype(F32)
    return high, mid, low


def copy_all(copies):
    for item in copies:
        item.start()
    for item in copies:
        item.wait()


def block_copies(blocks, scratch, sems, first):
    rows = scratch.shape[1] // 3
    return [
        pltpu.make_async_copy(
            block, scratch.at[:, pl.ds(at * rows, rows), :], sems.at[first + at]
        )
        for at, block in enumerate(blocks)
    ]


def slot_start(tile):
    return pl.multiple_of(tile * SLOT_TILE, SLOT_TILE)


def query_codes(fq, start, level=None):
    codes = fq[pl.ds(start, SLOT_TILE), :]
    codes = jnp.concatenate([codes, codes], axis=0)
    return codes if level is None else codes + level


def spread_stats(stats):
    wide = stats.astype(F32)
    rolled = pltpu.roll(wide, HEAD_DIM, 1)
    lower = lanes_of(stats.shape[0]) < HEAD_DIM
    level = jnp.where(lower, wide, rolled)
    delta = jnp.where(lower, rolled, wide)
    return level.astype(BF), delta.astype(BF)


def staged(items, begin, finish, ahead=2):
    held = []
    for item in items:
        held.append((item, begin(item)))
        if len(held) > ahead:
            finish(*held.pop(0))
    for entry in held:
        finish(*entry)


def projector(tok, lin, weights, bias):
    rows = 2 * SLOT_TILE

    def project(tile, carry):
        start = slot_start(tile)
        cells = dot_nn(both(tok, start, slice(0, tok.shape[2])), weights[...])
        cells = (cells + bias[0:1, :]).astype(BF)
        for part in range(3):
            cols = slice(part * WIDE, (part + 1) * WIDE)
            piece = cells[:, cols]
            if part == 0:
                piece = piece * (1.0 / math.sqrt(HEAD_DIM))
            for seg in range(2):
                lin[seg, pl.ds(start, SLOT_TILE), cols] = piece[
                    seg * SLOT_TILE : (seg + 1) * SLOT_TILE
                ]
        return carry

    return project


def make_queries(qa, lin, start, codes):
    rows = 2 * SLOT_TILE
    for head in range(GROUP):
        qa[head] = jnp.where(in_head(head, rows), both(lin, start, pair_cols(0, head)), codes)


def attend_step(qa, peak, acc, lin, start, code):
    rows = 2 * SLOT_TILE

    def begin(head):
        keys = both(lin, start, pair_cols(1, head))
        keys = jnp.where(in_head(head, rows), keys, code)
        return dot_nt(qa[head], keys)

    def finish(head, scores):
        vals = both(lin, start, pair_cols(2, head))
        vals = jnp.where(in_head(head, rows), vals, ones_row(head, rows))
        before = peak[head]
        top = jnp.maximum(before, jnp.max(scores, axis=1, keepdims=True))
        probs = jnp.exp(scores - jnp.concatenate([top] * (rows // LANES), axis=1))
        acc[head] = acc[head] * jnp.exp(before - top) + dot_nn(probs.astype(BF), vals)
        peak[head] = top

    staged(range(GROUP), begin, finish)


def head_lanes(lane, head):
    at = stat_lane(head)
    return (lane >= at) & (lane < at + 3)


def own_kernel(tiles, rng, bias, fq, fk, weights, tok, lin, acc_out, peak_out, qa, peak, acc):
    rows = 2 * SLOT_TILE
    lax.fori_loop(0, tiles, projector(tok, lin, weights, bias), 0)
    lane = lanes_of(rows)

    def per_tile(tile, carry):
        make_queries(qa, lin, slot_start(tile), query_codes(fq, slot_start(tile + tiles)))
        for head in range(GROUP):
            peak[head] = jnp.full((rows, LANES), FLOOR_MAX, F32)
            acc[head] = jnp.zeros((rows, LANES), F32)

        def step(other, inner):
            code = both(fk, slot_start(other + tiles), slice(0, LANES))
            attend_step(qa, peak, acc, lin, slot_start(other), code)
            return inner

        low = jnp.maximum(rng[2 * tile] - tiles, 0)
        high = jnp.minimum(rng[2 * tile + 1] - tiles, tiles)
        lax.fori_loop(low, high, step, 0)
        peaks = jnp.zeros((rows, LANES), F32)
        for head in range(GROUP):
            acc_out[tile, head] = acc[head]
            peaks = jnp.where(head_lanes(lane, head), peak[head], peaks)
        peak_out[tile] = peaks
        return carry

    lax.fori_loop(0, tiles, per_tile, 0)


def far_kernel(
    tiles, rng, bias, fq, fk, weights, before, after, lin, acc_in, peak_in,
    ctx_out, ctx_r_out, stat_out, lin_before, lin_after, qa, peak, acc,
):
    rows = 2 * SLOT_TILE
    lane = lanes_of(rows)
    lax.fori_loop(
        jnp.minimum(rng[0], tiles), tiles, projector(before, lin_before, weights, bias), 0
    )
    lax.fori_loop(
        0,
        jnp.maximum(rng[2 * tiles - 1] - 2 * tiles, 0),
        projector(after, lin_after, weights, bias),
        0,
    )

    def per_tile(tile, carry):
        first = slot_start(tile)
        low, high = rng[2 * tile], rng[2 * tile + 1]
        end_before = jnp.minimum(high, tiles)
        start_after = jnp.maximum(low - 2 * tiles, 0)
        end_after = high - 2 * tiles
        for head in range(GROUP):
            acc[head] = acc_in[tile, head]
            at = stat_lane(head)
            peak[head] = jnp.broadcast_to(peak_in[tile][:, at : at + 1], (rows, LANES))

        @pl.when((low < end_before) | (start_after < end_after))
        def _():
            make_queries(qa, lin, first, query_codes(fq, slot_start(tile + tiles)))

            def step_before(other, inner):
                code = both(fk, slot_start(other), slice(0, LANES))
                attend_step(qa, peak, acc, lin_before, slot_start(other), code)
                return inner

            def step_after(other, inner):
                code = both(fk, slot_start(other + 2 * tiles), slice(0, LANES))
                attend_step(qa, peak, acc, lin_after, slot_start(other), code)
                return inner

            lax.fori_loop(low, end_before, step_before, 0)
            lax.fori_loop(start_after, end_after, step_after, 0)

        totals = jnp.ones((rows, LANES), F32)
        peaks = jnp.zeros((rows, LANES), F32)
        for head in range(GROUP):
            mine = head_lanes(lane, head)
            totals = jnp.where(mine, acc[head], totals)
            peaks = jnp.where(mine, peak[head], peaks)
        totals = jnp.maximum(totals, 1.0)
        level = -(peaks + jnp.log(totals))
        level = jnp.where(lane < HEAD_DIM, level, 0.0) + pltpu.roll(
            jnp.where(lane < HEAD_DIM, 0.0, level), HEAD_DIM, 1
        )
        high_part, mid_part, low_part = three_parts(level)
        turn = (lane - STAT_LANE) % 3
        stats = jnp.where(turn == 0, high_part, jnp.where(turn == 1, mid_part, low_part))
        stats = stats.astype(BF)
        inverse = 1.0 / totals
        for pair in range(PAIRED):
            left, right = (
                acc[head] * inverse[:, stat_lane(head) : stat_lane(head) + 1]
                for head in (2 * pair, 2 * pair + 1)
            )
            cells = jnp.where(lane < HEAD_DIM, left, right)
            cols = slice(pair * LANES, (pair + 1) * LANES)
            for seg in range(2):
                part = cells[seg * SLOT_TILE : (seg + 1) * SLOT_TILE]
                ctx_out[seg, pl.ds(first, SLOT_TILE), cols] = part
                ctx_r_out[seg, pl.ds(first, SLOT_TILE), cols] = part.astype(BF)
        for seg in range(2):
            stat_out[seg, pl.ds(first, SLOT_TILE), :] = stats[seg * SLOT_TILE : (seg + 1) * SLOT_TILE]
        return carry

    lax.fori_loop(0, tiles, per_tile, 0)


def delta_kernel(d_ctx, ctx, stat, pay_out):
    rows = d_ctx.shape[1]
    lane = lanes_of(rows)
    for seg in range(2):
        stats = stat[seg].astype(F32)
        for pair in range(PAIRED):
            cols = slice(pair * LANES, (pair + 1) * LANES)
            cells = d_ctx[seg, :, cols]
            pay_out[seg, :, cols] = cells
            product = cells.astype(F32) * ctx[seg, :, cols]
            for half in range(2):
                head = 2 * pair + half
                keep = lane < HEAD_DIM if half == 0 else lane >= HEAD_DIM
                delta = -jnp.sum(jnp.where(keep, product, 0.0), axis=1, keepdims=True)
                for k, part in enumerate(three_parts(delta)):
                    at = HEAD_DIM + STAT_LANE + 3 * head + k
                    stats = jnp.where(lane == at, part, stats)
        pay_out[seg, :, WIDE : WIDE + LANES] = stats.astype(BF)


def backward_kernel(tiles, rng, fq, fk, *rest):
    pays, lins = rest[:3], rest[3:6]
    dlin_out, lin, pay, qa, da, ka, va, acc_q, acc_k, acc_v, sems = rest[6:]
    rows = 2 * SLOT_TILE
    copy_all(block_copies(pays, pay, sems, 0) + block_copies(lins, lin, sems, 3))
    acc_k[...] = jnp.zeros_like(acc_k)
    acc_v[...] = jnp.zeros_like(acc_v)

    def keys_of(start, code, head):
        keys = both(lin, start, pair_cols(1, head))
        return jnp.where(in_head(head, rows), keys, code + ones_row(head, rows))

    def vals_of(start, head):
        vals = both(lin, start, pair_cols(2, head))
        return jnp.where(in_head(head, rows), vals, ones_row(head, rows))

    def queries_of(start):
        level, delta = spread_stats(both(pay, start, slice(WIDE, WIDE + LANES)))
        return query_codes(fq, start, level), delta

    def per_tile(tile, carry):
        here = slot_start(tile + tiles)
        codes, delta = queries_of(here)
        code_a = both(fk, here, slice(0, LANES))
        for head in range(GROUP):
            mine = in_head(head, rows)
            qa[head] = jnp.where(mine, both(lin, here, pair_cols(0, head)), codes)
            da[head] = jnp.where(mine, both(pay, here, pair_cols(0, head)), delta)
            ka[head] = keys_of(here, code_a, head)
            va[head] = vals_of(here, head)
            acc_q[head] = jnp.zeros((rows, LANES), F32)
        low, high = rng[2 * tile], rng[2 * tile + 1]

        def own_step(other, inner):
            start = slot_start(other)
            at = other - tiles
            code = both(fk, start, slice(0, LANES))

            def begin(head):
                keys = keys_of(start, code, head)
                return keys, dot_nt(qa[head], keys), dot_nt(da[head], vals_of(start, head))

            def finish(head, state):
                keys, scores, d_probs = state
                probs = jnp.exp(scores)
                d_scores = (probs * d_probs).astype(BF)
                acc_q[head] += dot_nn(d_scores, keys)
                acc_k[at, head] += dot_tn(d_scores, qa[head])
                acc_v[at, head] += dot_tn(probs.astype(BF), da[head])

            staged(range(GROUP), begin, finish)
            return inner

        lax.fori_loop(jnp.maximum(low, tiles), jnp.minimum(high, 2 * tiles), own_step, 0)
        before = jnp.maximum(jnp.minimum(high, tiles) - low, 0)
        upper = jnp.maximum(low, 2 * tiles)
        after = jnp.maximum(high - upper, 0)

        def far_step(index, inner):
            other = jnp.where(index < before, low + index, upper + index - before)
            start = slot_start(other)
            code = both(fk, start, slice(0, LANES))
            codes_b, delta_b = queries_of(start)

            def begin(item):
                head, side = item
                if side == 0:
                    keys = keys_of(start, code, head)
                    return keys, dot_nt(qa[head], keys), dot_nt(da[head], vals_of(start, head))
                mine = in_head(head, rows)
                query = jnp.where(mine, both(lin, start, pair_cols(0, head)), codes_b)
                d_ctx = jnp.where(mine, both(pay, start, pair_cols(0, head)), delta_b)
                return (query, d_ctx), dot_nt(ka[head], query), dot_nt(va[head], d_ctx)

            def finish(item, state):
                head, side = item
                operand, scores, d_probs = state
                probs = jnp.exp(scores)
                d_scores = (probs * d_probs).astype(BF)
                if side == 0:
                    acc_q[head] += dot_nn(d_scores, operand)
                else:
                    query, d_ctx = operand
                    acc_k[tile, head] += dot_nn(d_scores, query)
                    acc_v[tile, head] += dot_nn(probs.astype(BF), d_ctx)

            staged([(head, side) for head in range(GROUP) for side in range(2)], begin, finish)
            return inner

        lax.fori_loop(0, before + after, far_step, 0)
        put(acc_q, None, slot_start(tile), 0, 1.0 / math.sqrt(HEAD_DIM))
        return carry

    def put(acc, tile, first, part, scale):
        lower = lanes_of(rows) < HEAD_DIM
        for pair in range(PAIRED):
            sides = [2 * pair, 2 * pair + 1]
            left, right = (acc[k] if tile is None else acc[tile, k] for k in sides)
            cells = jnp.where(lower, left, right) * scale
            cells = cells.astype(BF)
            cols = slice(part * WIDE + pair * LANES, part * WIDE + (pair + 1) * LANES)
            for seg in range(2):
                dlin_out[seg, pl.ds(first, SLOT_TILE), cols] = cells[
                    seg * SLOT_TILE : (seg + 1) * SLOT_TILE
                ]

    lax.fori_loop(0, tiles, per_tile, 0)

    def last(tile, carry):
        put(acc_k, tile, slot_start(tile), 1, 1.0)
        put(acc_v, tile, slot_start(tile), 2, 1.0)
        return carry

    lax.fori_loop(0, tiles, last, 0)


def attend_scratch():
    rows = 2 * SLOT_TILE
    return [
        pltpu.VMEM((GROUP, rows, LANES), BF),
        pltpu.VMEM((GROUP, rows, LANES), F32),
        pltpu.VMEM((GROUP, rows, LANES), F32),
    ]


def attend_own(tok, weights, bias, fq, fk, rng):
    slots = tok.shape[1]
    tiles = slots // SLOT_TILE
    rows = 2 * SLOT_TILE
    shapes = [
        ((2, slots, 3 * WIDE), BF),
        ((tiles, GROUP, rows, LANES), F32),
        ((tiles, rows, LANES), F32),
    ]
    return pl.pallas_call(
        functools.partial(own_kernel, tiles),
        out_shape=tuple(jax.ShapeDtypeStruct(shape, kind) for shape, kind in shapes),
        grid=(1,),
        in_specs=[SMEM] + [whole(item.shape) for item in (bias, fq, fk, weights, tok)],
        out_specs=tuple(whole(shape) for shape, _ in shapes),
        scratch_shapes=attend_scratch(),
        compiler_params=vmem(20),
        cost_estimate=cost(1, 1),
        name="attend_own",
    )(rng, bias, fq, fk, weights, tok)


def attend_far(before, after, own, weights, bias, fq, fk, rng):
    slots = before.shape[1]
    tiles = slots // SLOT_TILE
    shapes = [
        ((2, slots, WIDE), F32),
        ((2, slots, WIDE), BF),
        ((2, slots, LANES), BF),
        ((2, slots, 3 * WIDE), BF),
        ((2, slots, 3 * WIDE), BF),
    ]
    return pl.pallas_call(
        functools.partial(far_kernel, tiles),
        out_shape=tuple(jax.ShapeDtypeStruct(shape, kind) for shape, kind in shapes),
        grid=(1,),
        in_specs=[SMEM]
        + [whole(item.shape) for item in (bias, fq, fk, weights, before, after, *own)],
        out_specs=tuple(whole(shape) for shape, _ in shapes),
        scratch_shapes=attend_scratch(),
        compiler_params=vmem(32),
        cost_estimate=cost(4, 8),
        name="attend_far",
    )(rng, bias, fq, fk, weights, before, after, *own)


def attend_back(lins, pays, fq, fk, rng):
    slots = pays[1].shape[1]
    tiles = slots // SLOT_TILE
    rows = 2 * SLOT_TILE
    return pl.pallas_call(
        functools.partial(backward_kernel, tiles),
        out_shape=jax.ShapeDtypeStruct((2, slots, 3 * WIDE), BF),
        grid=(1,),
        in_specs=[SMEM, whole(fq.shape), whole(fk.shape)] + [ANY] * 6,
        out_specs=whole((2, slots, 3 * WIDE)),
        scratch_shapes=[
            pltpu.VMEM((2, 3 * slots, 3 * WIDE), BF),
            pltpu.VMEM((2, 3 * slots, WIDE + LANES), BF),
            pltpu.VMEM((GROUP, rows, LANES), BF),
            pltpu.VMEM((GROUP, rows, LANES), BF),
            pltpu.VMEM((GROUP, rows, LANES), BF),
            pltpu.VMEM((GROUP, rows, LANES), BF),
            pltpu.VMEM((GROUP, rows, LANES), F32),
            pltpu.VMEM((tiles, GROUP, rows, LANES), F32),
            pltpu.VMEM((tiles, GROUP, rows, LANES), F32),
            pltpu.SemaphoreType.DMA((6,)),
        ],
        compiler_params=vmem(32),
        cost_estimate=cost(24, 12),
        name="attend_back",
    )(rng, fq, fk, *pays, *lins)


def payload(d_ctx, ctx, stat):
    slots = d_ctx.shape[1]
    return pl.pallas_call(
        delta_kernel,
        out_shape=jax.ShapeDtypeStruct((2, slots, WIDE + LANES), BF),
        grid=(1,),
        in_specs=[whole(d_ctx.shape), whole(ctx.shape), whole(stat.shape)],
        out_specs=whole((2, slots, WIDE + LANES)),
        compiler_params=vmem(10),
        cost_estimate=cost(0.5, 3),
        name="payload",
    )(d_ctx, ctx, stat)


def norm_forward(hidden):
    mean_val = jnp.mean(hidden, axis=-1, keepdims=True)
    centred = hidden - mean_val
    rate = lax.rsqrt(jnp.mean(centred * centred, axis=-1, keepdims=True) + EPS)
    return centred * rate, rate


def norm_backward(d_normal, normal, rate):
    return rate * (
        d_normal
        - jnp.mean(d_normal, axis=-1, keepdims=True)
        - normal * jnp.mean(d_normal * normal, axis=-1, keepdims=True)
    )


def normal_share(values):
    bell = jnp.exp(values * values * -0.5)
    t = 1.0 / (1.0 + (0.3275911 / math.sqrt(2.0)) * jnp.abs(values))
    poly = 0.5 * 1.061405429
    for term in (-1.453152027, 1.421413741, -0.284496736, 0.254829592):
        poly = poly * t + 0.5 * term
    beyond = poly * t * bell
    share = jnp.where(values < 0.0, beyond, 1.0 - beyond)
    return share, bell * (1.0 / math.sqrt(2.0 * math.pi))


def chain_kernel(
    tok, ctx_a, ctx_b, cot, wo_a, wo_b, vecs, up, up_bias, down,
    out, d_first_out, d_ctx_a, d_ctx_b, act_out, d_pre_out, normed_out, d_down_out, d_attn_out,
    sums, up_sums, slope,
):
    hidden = up.shape[1]
    chunk = min(512, hidden)

    @pl.when(pl.program_id(0) == 0)
    def _():
        sums[...] = jnp.zeros_like(sums)
        up_sums[...] = jnp.zeros_like(up_sums)

    out_bias, gain_1, shift_1, down_bias, gain_2, shift_2 = (vecs[k : k + 1, :] for k in range(6))

    def tally(row, cells):
        sums[row : row + 1, :] += jnp.sum(cells, axis=0, keepdims=True)

    first = (
        tok[0, 0].astype(F32)
        + (dot_nn(ctx_a[...], wo_a[...]) + dot_nn(ctx_b[...], wo_b[...]))
        + out_bias
    )
    normal_1, rate_1 = norm_forward(first)
    normed = normal_1 * gain_1 + shift_1
    normed_r = normed.astype(BF)
    normed_out[...] = normed_r
    second = [normed + down_bias]

    def columns(part):
        return slice(part * chunk, (part + 1) * chunk)

    def begin_up(part):
        return dot_nn(normed_r, up[:, columns(part)])

    def finish_up(part, lin):
        cols = columns(part)
        pre = lin + up_bias[:, cols]
        share, bell = normal_share(pre)
        slope[:, cols] = share + pre * bell
        act_r = (pre * share).astype(BF)
        act_out[:, cols] = act_r
        second[0] = second[0] + dot_nn(act_r, down[cols, :])

    staged(range(hidden // chunk), begin_up, finish_up, 1)
    second = second[0]
    normal_2, rate_2 = norm_forward(second)
    out[...] = (normal_2 * gain_2 + shift_2).astype(BF)
    d_out = cot[0, 0].astype(F32)
    tally(4, d_out * normal_2)
    tally(5, d_out)
    d_second = norm_backward(d_out * gain_2, normal_2, rate_2)
    tally(3, d_second)
    d_down_r = d_second.astype(BF)
    d_down_out[...] = d_down_r
    d_normed = [d_second]

    def begin_down(part):
        return dot_nt(d_down_r, down[columns(part), :])

    def finish_down(part, d_act):
        cols = columns(part)
        d_pre_r = (d_act * slope[:, cols]).astype(BF)
        d_pre_out[:, cols] = d_pre_r
        up_sums[0:1, cols] += jnp.sum(d_pre_r.astype(F32), axis=0, keepdims=True)
        d_normed[0] = d_normed[0] + dot_nt(d_pre_r, up[:, cols])

    staged(range(hidden // chunk), begin_down, finish_down, 1)
    d_normed = d_normed[0]
    tally(1, d_normed * normal_1)
    tally(2, d_normed)
    d_first = norm_backward(d_normed * gain_1, normal_1, rate_1)
    tally(0, d_first)
    d_first_out[...] = d_first
    d_attn_r = d_first.astype(BF)
    d_attn_out[...] = d_attn_r
    d_ctx_a[...] = dot_nt(d_attn_r, wo_a[...]).astype(BF)
    d_ctx_b[...] = dot_nt(d_attn_r, wo_b[...]).astype(BF)


def chain(micro, tokens, ctx_a, ctx_b, cotangent, wo_a, wo_b, vecs, up, up_bias, down):
    slots, model = tokens.shape[2:]
    hidden = up.shape[1]
    rows = min(CHAIN_ROWS, slots)
    of_micro = pl.BlockSpec((1, 1, rows, model), lambda i: (micro, 0, i, 0))
    sizes = [
        (model, BF), (model, F32), (WIDE, BF), (WIDE, BF), (hidden, BF), (hidden, BF),
        (model, BF), (model, BF), (model, BF),
    ]
    return pl.pallas_call(
        chain_kernel,
        out_shape=tuple(jax.ShapeDtypeStruct((slots, cols), kind) for cols, kind in sizes)
        + (jax.ShapeDtypeStruct((8, model), F32), jax.ShapeDtypeStruct((8, hidden), F32)),
        grid=(slots // rows,),
        in_specs=[
            of_micro,
            row_block(rows, WIDE),
            row_block(rows, WIDE),
            of_micro,
            whole(wo_a.shape),
            whole(wo_b.shape),
            whole(vecs.shape),
            whole(up.shape),
            whole(up_bias.shape),
            whole(down.shape),
        ],
        out_specs=tuple(row_block(rows, cols) for cols, _ in sizes)
        + (whole((8, model)), whole((8, hidden))),
        scratch_shapes=[pltpu.VMEM((rows, hidden), F32)],
        compiler_params=vmem(28),
        cost_estimate=cost(6, 12),
        name="chain",
    )(tokens, ctx_a, ctx_b, cotangent, wo_a, wo_b, vecs, up, up_bias, down)


def weight_kernel(*refs):
    acts, d_downs, normeds, d_pres, d_attns, ctx_as, ctx_bs, sums, up_sums = (
        refs[2 * k : 2 * k + 2] for k in range(9)
    )
    seg, out = refs[18], refs[19]
    step = pl.program_id(0)
    width = out.shape[1]
    parts = up_sums[0].shape[1] // width

    def summed(lefts, rights):
        left = jnp.concatenate([item[...] for item in lefts], axis=0)
        return dot_tn(left, jnp.concatenate([item[...] for item in rights], axis=0)).astype(BF)

    @pl.when(step < parts)
    def _():
        out[...] = summed(acts, d_downs)

    @pl.when((step >= parts) & (step < 2 * parts))
    def _():
        out[...] = summed(normeds, d_pres)

    @pl.when((step == 2 * parts) & (seg[0] == 0))
    def _():
        out[:WIDE, :] = summed(ctx_as, d_attns)
        out[WIDE:, :] = summed(ctx_bs, d_attns)

    @pl.when((step == 2 * parts) & (seg[0] != 0))
    def _():
        out[:WIDE, :] = summed(ctx_bs, d_attns)
        out[WIDE:, :] = summed(ctx_as, d_attns)

    @pl.when(step == 2 * parts + 1)
    def _():
        wide = up_sums[0][0:1, :] + up_sums[1][0:1, :]
        cells = [sums[0][...] + sums[1][...]]
        cells += [wide[:, k * width : (k + 1) * width] for k in range(parts)]
        cells += [jnp.zeros((width - 8 - parts, width), F32)]
        out[...] = jnp.concatenate(cells, axis=0).astype(BF)


def weight_grads(groups, seg, model):
    flat = [item for group in groups for item in group]
    slots, hidden = groups[0][0].shape
    parts = hidden // model

    def fixed(item):
        return pl.BlockSpec(item.shape, lambda i: (0, 0))

    def column(first):
        return pl.BlockSpec((slots, model), lambda i: (0, jnp.clip(i - first, 0, parts - 1)))

    specs = [column(0)] * 2
    specs += [fixed(item) for item in groups[1] + groups[2]]
    specs += [column(parts)] * 2
    specs += [fixed(item) for group in groups[4:] for item in group]
    return pl.pallas_call(
        weight_kernel,
        out_shape=pltpu.HBM(((2 * parts + 1) * model + 16, model), BF),
        grid=(2 * parts + 2,),
        in_specs=specs + [SMEM],
        out_specs=row_block(model, model),
        compiler_params=vmem(24),
        cost_estimate=cost(1, 2),
        name="weight_grads",
    )(*flat, seg)


def unpack_kernel(parts, cells, down_out, up_out, out_out):
    step = pl.program_id(0)

    @pl.when(step < parts)
    def _():
        down_out[...] = cells[...].astype(F32)

    @pl.when((step >= parts) & (step < 2 * parts))
    def _():
        up_out[...] = cells[...].astype(F32)

    @pl.when(step == 2 * parts)
    def _():
        out_out[...] = cells[...].astype(F32)


def unpack(cells, hidden):
    model = cells.shape[1]
    parts = hidden // model
    block = (model, model)
    return pl.pallas_call(
        functools.partial(unpack_kernel, parts),
        out_shape=(
            jax.ShapeDtypeStruct((hidden, model), F32),
            jax.ShapeDtypeStruct((model, hidden), F32),
            jax.ShapeDtypeStruct((model, model), F32),
        ),
        grid=(2 * parts + 1,),
        in_specs=[pl.BlockSpec(block, lambda i: (i, 0))],
        out_specs=(
            pl.BlockSpec(block, lambda i: (jnp.minimum(i, parts - 1), 0)),
            pl.BlockSpec(block, lambda i: (0, jnp.clip(i - parts, 0, parts - 1))),
            pl.BlockSpec(block, lambda i: (0, 0)),
        ),
        compiler_params=vmem(12),
        cost_estimate=cost(0.1, 16),
        name="unpack",
    )(cells)


def qkv_weight_kernel(micros, *refs):
    joints, d_lins, out = refs[:micros], refs[micros : 2 * micros], refs[-1]
    slots, model = joints[0].shape[1:]
    total = jnp.zeros((model, WIDE), F32)
    sums = jnp.zeros((1, WIDE), F32)
    for m in range(micros):
        for seg in range(2):
            cells = d_lins[m][seg]
            total = total + dot_tn(joints[m][seg], cells)
            sums = sums + jnp.sum(cells.astype(F32), axis=0, keepdims=True)
    out[:model, :] = total.astype(BF)
    first = lax.broadcasted_iota(jnp.int32, (16, WIDE), 0) == 0
    out[model : model + 16, :] = jnp.where(first, sums, 0.0).astype(BF)
    if out.shape[0] > model + 16:
        out[model + 16 :, :] = jnp.zeros((out.shape[0] - model - 16, WIDE), BF)


def qkv_weight_grad(joints, d_lins, after, rows):
    slots, model = joints[0].shape[1:]
    return pl.pallas_call(
        functools.partial(qkv_weight_kernel, len(joints)),
        out_shape=jax.ShapeDtypeStruct((rows, 3 * WIDE), BF),
        grid=(3,),
        in_specs=[pl.BlockSpec((2, slots, model), lambda i: (0, 0, 0))] * len(joints)
        + [pl.BlockSpec((2, slots, WIDE), lambda i: (0, 0, i))] * len(joints)
        + [ANY],
        out_specs=pl.BlockSpec((rows, WIDE), lambda i: (0, i)),
        compiler_params=vmem(20),
        cost_estimate=cost(1.6, 4),
        name="qkv_weight_grad",
    )(*joints, *d_lins, after)


def finish_kernel(cells, *refs):
    micros = (len(refs) - 3) // 2
    near, far = refs[:micros], refs[micros : 2 * micros]
    out, small, token_out = refs[2 * micros :]
    rows = out.shape[0]
    for seg in range(2):
        for part in range(3):
            first = (2 * part + seg) * WIDE
            block = cells[seg, :rows, part * WIDE : (part + 1) * WIDE]
            out[:, first : first + WIDE] = block.astype(F32)
    edge = cells[:, rows : rows + 16, :].astype(F32)
    small[...] = jnp.concatenate(
        [edge[seg, :, part * WIDE : (part + 1) * WIDE] for part in (0, 2) for seg in range(2)],
        axis=1,
    )
    for m in range(micros):
        token_out[m, 0] = near[m][...] + far[m][...].astype(F32)


def finish(cells, near, far):
    slots, model = near[0].shape
    shapes = [
        ((model, 6 * WIDE), F32),
        ((16, 4 * WIDE), F32),
        ((len(near), 1, slots, model), F32),
    ]
    flat = [cells, *near, *far]
    return pl.pallas_call(
        finish_kernel,
        out_shape=tuple(jax.ShapeDtypeStruct(shape, kind) for shape, kind in shapes),
        grid=(1,),
        in_specs=[whole(item.shape) for item in flat],
        out_specs=tuple(whole(shape) for shape, _ in shapes),
        compiler_params=vmem(28),
        cost_estimate=cost(0.1, 12),
        name="finish",
    )(*flat)


def swapped(value):
    return lax.ppermute(value, "seg", [(0, 1), (1, 0)])


def shifted(value, by):
    size = lax.axis_size("seq")
    return lax.ppermute(
        value, "seq", [(i, i + by) for i in range(size) if 0 <= i + by < size]
    )


def flipped(value, bit):
    return lax.ppermute(value, "seq", [(i, i ^ bit) for i in range(lax.axis_size("seq"))])


def pick(value, index, axis):
    zero = jnp.int32(0)
    starts = [zero] * value.ndim
    starts[axis] = lax.convert_element_type(index, jnp.int32)
    sizes = list(value.shape)
    sizes[axis] = 1
    part = lax.dynamic_slice(value, starts, sizes)
    return lax.reshape(part, value.shape[:axis] + value.shape[axis + 1 :])


def stacked(pieces):
    return lax.concatenate([lax.expand_dims(piece, (0,)) for piece in pieces], 0)


def by_segment(mine, other, seg):
    return lax.select(seg == 0, stacked([mine, other]), stacked([other, mine]))


def bit_groups(size):
    bits = size.bit_length() - 1
    groups = [(k, 1) for k in range(min(bits, 2))]
    groups += [(k, min(2, bits - k)) for k in range(2, bits, 2)]
    return groups


def moved(value, seg_flip, seq_flip):
    size = lax.axis_size("seq")
    total = size * lax.axis_size("seg")
    pairs = [(i, i ^ (seg_flip * size + seq_flip)) for i in range(total)]
    return lax.ppermute(value, ("seg", "seq"), pairs)


def scatter_seq(cells, seq):
    for shift, count in bit_groups(lax.axis_size("seq")):
        own = lax.bitwise_and(lax.shift_right_logical(seq, jnp.int32(shift)), jnp.int32(2**count - 1))
        split = cells.reshape((-1, 2**count) + cells.shape[1:])
        total = pick(split, own, 1).astype(F32)
        for turn in range(1, 2**count):
            total = total + moved(pick(split, own ^ turn, 1), 0, turn << shift).astype(F32)
        cells = total.astype(BF)
    return cells


def merged(cells, first, second):
    order = [k for k in range(cells.ndim) if k != first]
    order.insert(second, first)
    shape = [cells.shape[k] for k in order]
    if cells.shape[order[second - 1]] > 1:
        cells = lax.transpose(cells, order)
    shape[second - 1 : second + 1] = [shape[second - 1] * shape[second]]
    return lax.reshape(cells, shape)


def in_order(pieces, own):
    bit = 1
    pieces = list(pieces)
    while bit < len(pieces):
        turned = lax.ne(lax.bitwise_and(own, jnp.int32(bit)), jnp.int32(0))
        pieces = [
            lax.select(turned, pieces[k ^ bit], pieces[k]) for k in range(len(pieces))
        ]
        bit *= 2
    return stacked(pieces)


def gather_all(cells, seg, seq):
    groups = bit_groups(lax.axis_size("seq"))[::-1]
    for at, (shift, count) in enumerate(groups):
        turns = [turn << shift for turn in range(2**count)]
        own = lax.bitwise_and(lax.shift_right_logical(seq, jnp.int32(shift)), jnp.int32(2**count - 1))
        if at == max(len(groups) - 2, 0):
            sides = [
                in_order([moved(cells, g, t) if g or t else cells for t in turns], own)
                for g in range(2)
            ]
            cells = merged(in_order(sides, seg), 1, 2)
        else:
            pieces = in_order([moved(cells, 0, t) if t else cells for t in turns], own)
            cells = merged(pieces, 0, cells.ndim - 2)
    return cells


def code_tables(lengths, base, slots, extent):
    spans = jnp.maximum(lengths[:, 0], lengths[:, 1])
    count = spans.shape[1]
    order = jnp.arange(count, dtype=jnp.int32)
    ends = jnp.sum(jnp.where(order[None, :] <= order[:, None], spans[:, None, :], 0), axis=2)
    place = base + jnp.arange(extent, dtype=jnp.int32)
    past = ends[:, None, :] <= place[None, :, None]
    pair = jnp.sum(past.astype(jnp.int32), axis=2)
    start = jnp.sum(jnp.where(past, spans[:, None, :], 0), axis=2)
    here = order[None, None, :] == pair[:, :, None]
    stop = jnp.sum(jnp.where(here, ends[:, None, :], 0), axis=2)
    inside = (pair < count) & (place >= 0)[None, :]
    counts = [jnp.sum(jnp.where(here, lengths[:, c, None, :], 0), axis=2) for c in range(2)]
    valid = jnp.stack(
        [inside & (place[None, :] - start < counts[c]) for c in range(2)], axis=1
    )
    lane = jnp.arange(LANES, dtype=jnp.int32) % HEAD_DIM
    digits = [pair, pair // DIGIT, pair // (DIGIT * DIGIT)]
    hot = jnp.zeros(pair.shape + (LANES,), bool)
    for k, digit in enumerate(digits):
        hot = hot | (lane == (digit % DIGIT)[:, :, None] + k * DIGIT)
    hot = hot & inside[:, :, None]
    is_code = lane <= BAD_LANE
    fq = jnp.where(is_code & ~hot, MASK_OFF, 0.0).astype(BF)
    bad = (lane == BAD_LANE) & ~valid[:, :, :, None]
    fk = (hot[:, None] | bad).astype(BF)
    low = jnp.where(inside, start, place[None, :])
    high = jnp.where(inside, stop, place[None, :])
    first = extent // 3
    low = jnp.clip(low[:, first : first + slots : SLOT_TILE] - base, 0, extent)
    last = first + SLOT_TILE - 1
    high = jnp.clip(high[:, last : first + slots : SLOT_TILE] - base, 0, extent)
    rng = jnp.stack([low // SLOT_TILE, -(-high // SLOT_TILE)], axis=2)
    return fq, fk, rng.reshape(rng.shape[0], -1).astype(jnp.int32)


def second_half(seg, seq, pays, forwards, owns, fq, fk, rng, joint, own_cols, d_firsts):
    micros = len(pays)
    ring = lax.axis_size("seq")
    slots, model = joint[0].shape[1:]
    d_lins, near, far = [], [], []
    pays = [*pays[:-1], (shifted(pays[-1], 1), pays[-1], shifted(pays[-1], -1))]
    for m in range(micros):
        lins = (forwards[m][3], owns[m][0], forwards[m][4])
        d_lin = attend_back(lins, pays[m], fq[m], fk[m], rng[m])
        d_lins.append(d_lin)
        far.append(swapped(dot_nt(pick(d_lin, 1 - seg, 0), own_cols).astype(BF)))
        near.append(d_firsts[m] + dot_nt(pick(d_lin, seg, 0), own_cols))
    late = model + 8 * max(ring, 16)
    qkv = qkv_weight_grad(joint, d_lins, far[0], late).reshape(ring, late // ring, 3 * WIDE)
    qkv = scatter_seq(qkv, seq)
    qkv, far[-1], near[-1] = lax.optimization_barrier((qkv, far[-1], near[-1]))
    qkv = gather_all(qkv, seg, seq).reshape(2, late, 3 * WIDE)
    qkv_grad, late_sums, token_grads = finish(qkv, near, far)
    return token_grads, qkv_grad, late_sums


def per_device(
    tokens,
    lengths,
    qkv_weight,
    query_bias,
    value_bias,
    out_weight,
    out_bias,
    attn_gain,
    attn_shift,
    up_weight,
    up_bias,
    down_weight,
    down_bias,
    ffn_gain,
    ffn_shift,
    cotangent,
):
    seg = lax.axis_index("seg")
    seq = lax.axis_index("seq")
    ring = lax.axis_size("seq")
    micros, _, slots, model = tokens.shape
    hidden = up_weight.shape[1]
    extent = 3 * slots
    mine = [tokens[m, 0] for m in range(micros)]
    joint = []
    partner = None
    for m in range(micros):
        sent = mine[m]
        if m:
            sent, partner = lax.optimization_barrier((sent, partner))
            joint[-1] = by_segment(mine[m - 1], partner, seg)
        partner = swapped(sent)
        joint.append(by_segment(sent, partner, seg))
    before, after = [], []
    fq, fk, rng = code_tables(lengths, seq * slots - slots, slots, extent)
    own_cols = pick(qkv_weight.reshape(model, 3, 2, WIDE), seg, 2).reshape(model, 3 * WIDE)
    own_bias = jnp.concatenate(
        [
            pick(query_bias.reshape(2, WIDE), seg, 0),
            jnp.zeros((WIDE,), query_bias.dtype),
            pick(value_bias.reshape(2, WIDE), seg, 0),
        ]
    ).astype(F32)
    own_bias = jnp.broadcast_to(own_bias, (8, 3 * WIDE))
    halves = out_weight.reshape(2, WIDE, model)
    wo_a, wo_b = pick(halves, seg, 0), pick(halves, 1 - seg, 0)
    vecs = jnp.stack(
        [out_bias, attn_gain, attn_shift, down_bias, ffn_gain, ffn_shift, out_bias, out_bias]
    ).astype(F32)
    up_row = up_bias.astype(F32)[None, :]
    before.append(shifted(joint[0], 1))
    after.append(shifted(joint[0], -1))
    owns = [attend_own(joint[m], own_cols, own_bias, fq[m], fk[m], rng[m]) for m in range(micros)]
    for m in range(1, micros):
        sent, before[-1], after[-1], owns = lax.optimization_barrier(
            (joint[m], before[-1], after[-1], owns)
        )
        before.append(shifted(sent, 1))
        after.append(shifted(sent, -1))
    forwards = [
        attend_far(before[m], after[m], owns[m], own_cols, own_bias, fq[m], fk[m], rng[m])
        for m in range(micros)
    ]
    chains, contexts = [], []
    for m in range(micros):
        ctx_r = forwards[m][1]
        contexts.append((pick(ctx_r, seg, 0), swapped(pick(ctx_r, 1 - seg, 0))))
    contexts[0], forwards = lax.optimization_barrier((contexts[0], forwards))
    for m in range(micros):
        chains.append(
            chain(
                m, tokens, *contexts[m], cotangent, wo_a, wo_b, vecs, up_weight, up_row, down_weight
            )
        )
    def paid(m, arrived):
        return payload(by_segment(chains[m][2], arrived, seg), forwards[m][0], forwards[m][2])

    arrived = [swapped(item[3]) for item in chains]
    pays = [paid(m, arrived[m]) for m in range(micros - 1)]
    columns = [[item[k] for item in chains] for k in range(len(chains[0]))]
    columns[4], pays = lax.optimization_barrier((columns[4], pays))
    grads = weight_grads(
        [columns[4], columns[7], columns[6], columns[5], columns[8]]
        + [[c[0] for c in contexts], [c[1] for c in contexts]]
        + [columns[9], columns[10]],
        jnp.reshape(seg, (1,)).astype(jnp.int32),
        model,
    )
    pays = [(shifted(pay, 1), pay, shifted(pay, -1)) for pay in pays]
    grads, late, pays = lax.optimization_barrier((grads, arrived[-1], pays))
    grads = lax.psum(grads, ("seg", "seq"))
    pays.append(paid(micros - 1, late))
    d_firsts = [item[1] for item in chains]
    given = (pays, forwards, owns, fq, fk, rng, joint, own_cols, d_firsts)

    def taken(given):
        return second_half(seg, seq, *given)

    def empty(given):
        shapes = jax.eval_shape(taken, given)
        return jax.tree.map(lambda item: jnp.zeros(item.shape, item.dtype), shapes)

    token_grads, qkv_grad, late_sums = lax.cond(lengths[0, 0, 0] >= 0, taken, empty, given)
    down_grad, up_grad, out_grad = unpack(grads, hidden)
    tail = grads[2 * hidden + model : 2 * hidden + model + 16].astype(F32)
    return (
        jnp.stack([item[0] for item in chains])[:, None],
        token_grads,
        qkv_grad,
        late_sums[0, :model],
        late_sums[0, model:],
        out_grad,
        tail[0],
        tail[1],
        tail[2],
        up_grad,
        tail[8 : 8 + hidden // model].reshape(-1),
        down_grad,
        tail[3],
        tail[4],
        tail[5],
    )


def solution(mesh):
    split = P(None, "seg", "seq", None)
    return jax.shard_map(
        per_device,
        mesh=mesh,
        in_specs=(split,) + (P(),) * 14 + (split,),
        out_specs=(split, split) + (P(),) * 13,
        check_vma=False,
    )
```

time: 1860 us -> 340 us (0.18)
  blocking collectives: 812 us -> 0 us
  matrix products: 359 us -> 6.96 us
  local copies, waits for them, and re-layouts: 319 us -> 28.6 us
  Pallas kernels: 0 us -> 130 us
  other arithmetic: 140 us -> 22.4 us
  waiting for transfers between devices: 139 us -> 60.5 us
    unnamed x1 -> x0, blocking collectives: 812 us -> none
    dot_general x108 -> x4, matrix products: 359 us -> 6.96 us  [dot_nt(): lax.dot_general(left, right, (((1,), (1,)), ((), ())), preferred_element_...]
    pallas_call x0 -> x14, Pallas kernels: none -> 130 us  [the longest x2 39.3 us: attend_back(): pl.pallas_call(functools.partial(backward_kernel, tiles), out_shape=jax.S...]
    unnamed x508 -> x67, local copies, waits for them, and re-layouts: 116 us -> 12.2 us
    slice x49 -> x8, local copies, waits for them, and re-layouts: 93.5 us -> 2.82 us  [the longest x1 1.32 us: per_device(): late_sums[0, model:]]
    all_gather x1 -> x0, waiting for transfers between devices: 85.5 us -> none  [per_device(): lax.all_gather(grad_share.astype(jnp.bfloat16), ('seg', 'seq'), axis=0, t...]
    reshape x6 -> x8, local copies, waits for them, and re-layouts: 75.5 us -> 2.04 us  [the longest x6 2.01 us: pick(): return lax.reshape(part, value.shape[:axis] + value.shape[axis + 1:])]
    concatenate x9 -> x4, other arithmetic: 48.9 us -> 3.3 us  [stacked(): lax.concatenate([lax.expand_dims(piece, (0,)) for piece in pieces], 0)]
  transfers between devices with their start and end apart: 13 -> 29, of which waited for: 4 -> 15; matrix products, arithmetic and copies ran while one was open for 13% -> 11% of each run, Pallas kernels for 0% -> 30%
where the time goes in v1:
time: 340 us; the launch traced here: 338 us
  Pallas kernels  130 us (38%)
  starting transfers between devices  73.6 us (22%)
  waiting for transfers between devices  60.5 us (18%)
  local copies, waits for them, and re-layouts  28.6 us (8%)
  other arithmetic  22.4 us (7%)
  between operations  15.4 us (5%)
  matrix products  6.96 us (2%)
    ppermute x8, starting transfers between devices, shifted(): lax.ppermute(value, 'seq', [(i, i + by) for i in range(size) if 0 <= i +...  41.5 us
    pallas_call x2, Pallas kernels, attend_back(): pl.pallas_call(functools.partial(backward_kernel, tiles), out_shape=jax.S...  39.3 us
    ppermute x12, waiting for transfers between devices, moved(): return lax.ppermute(value, ('seg', 'seq'), pairs)  28.7 us
    pallas_call x2, Pallas kernels, attend_own(): pl.pallas_call(functools.partial(own_kernel, tiles), out_shape=tuple((jax...  25.9 us
    psum x1, waiting for transfers between devices, per_device(): grads = lax.psum(grads, ('seg', 'seq'))  24.5 us
    pallas_call x2, Pallas kernels, chain(): pl.pallas_call(chain_kernel, out_shape=tuple((jax.ShapeDtypeStruct((slots...  23 us
    ppermute x12, starting transfers between devices, moved(): return lax.ppermute(value, ('seg', 'seq'), pairs)  21.4 us
    pallas_call x2, Pallas kernels, attend_far(): pl.pallas_call(functools.partial(far_kernel, tiles), out_shape=tuple((jax...  16.1 us
  transfers between devices with their start and end apart: 29, of which 15 were waited for; matrix products, arithmetic and copies ran while one was open for 11% of the time, Pallas kernels for 30%

profile of v1, /device:TPU:0, one launch (start us, length us, event | category | flops | bytes accessed | tf_op | source)
XLA Modules:
  0.0 337.5 jit_solution(15065371557898313548)
XLA Ops:
  7.3 2.4 slice_bitcast_fusion.7
  9.7 2.9 collective-permute-start.16
  14.7 2.3 or_and_fusion
  17.0 4.0 %select_convert_fusion = bf16[2,1536,128]{2,1,0:T(8,128)(2,1)} fusion(pred[128]{0:T(512)(128)(4,1)S(1)} %get-tuple-element.438, pred[2,1536]{1,0:T(4,128)(4,1)S(1)} %get-tuple-element.429, s32[2,1536]{1,0:T(2,128)S(1)} %get-tuple-element.426, s32[2,1536]{1,0:T(2,128)S(1)} %get-tuple-element.427, s32[2,1536]{1,0:T(2,128)S(1)} %get-tuple-element.425, ...), kind=kLoop, calls=%fused_computation.52 | loop fusion | flops 3932160 | bytes 827008 | tf_op jit(solution)/shard_map/convert_element_type | solution.py:980
  21.0 1.6 copy.92
  22.6 1.1 or_convert_fusion
  24.9 2.5 maximum_select_fusion.1.tok
  27.4 1.3 collective-permute-start.19
  28.7 4.0 %collective-permute-start.18 = (bf16[2,512,512]{2,1,0:T(8,128)(2,1)}, bf16[2,512,512]{2,1,0:T(8,128)(2,1)}, u32[]{:S(2)}, u32[]{:S(2)}) collective-permute-start(bf16[2,512,512]{2,1,0:T(8,128)(2,1)} %maximum_select_fusion.1.tok), channel_id=1, source_target_pairs={{0,1},{1,2},{2,3},{3,4},{4,5},{5,6},{6,7},{7,8},{8,9},{9,10},{10,1... | collective-permute-start | bytes 3145736 | tf_op jit(solution)/shard_map/ppermute | solution.py:866
  33.6 1.6 collective-permute-start.17
  35.2 1.2 slice_bitcast_fusion.10
  36.4 11.7 %attend_own.2 = (bf16[2,512,768]{2,1,0:T(8,128)(2,1)}, f32[4,4,256,128]{3,2,1,0:T(8,128)S(1)}, f32[4,256,128]{2,1,0:T(8,128)S(1)}) custom-call(s32[8]{0:T(128)S(1)} %squeeze.81.rng, f32[8,768]{1,0:T(8,128)S(1)} %broadcast_in_dim.170.bias, bf16[1536,128]{1,0:T(8,128)(2,1)S(1)} %get-tuple-element.409.fq, bf16[2,1536,128]{2,1,0:T(8,128)(2,1)S(1)} %get-tuple-element.404.fk, ...), custom_call_target="tpu_custom_call" | custom-call | flops 1000000000 | bytes 1000000 | tf_op jit(solution)/shard_map/attend_own/pallas_call | solution.py:461
  49.0 1.2 maximum_select_fusion.tok
  50.7 14.1 %attend_own.3 = (bf16[2,512,768]{2,1,0:T(8,128)(2,1)}, f32[4,4,256,128]{3,2,1,0:T(8,128)S(1)}, f32[4,256,128]{2,1,0:T(8,128)S(1)}) custom-call(s32[8]{0:T(128)S(1)} %squeeze.86.rng, f32[8,768]{1,0:T(8,128)S(1)} %broadcast_in_dim.170.bias, bf16[1536,128]{1,0:T(8,128)(2,1)S(1)} %get-tuple-element.410.fq, bf16[2,1536,128]{2,1,0:T(8,128)(2,1)S(1)} %get-tuple-element.405.fk, ...), custom_call_target="tpu_custom_call" | custom-call | flops 1000000000 | bytes 1000000 | tf_op jit(solution)/shard_map/attend_own/pallas_call | solution.py:461
  64.8 1.3 copy-done.9
  66.9 1.3 collective-permute-start.22
  68.2 4.0 %collective-permute-start.21 = (bf16[2,512,512]{2,1,0:T(8,128)(2,1)}, bf16[2,512,512]{2,1,0:T(8,128)(2,1)}, u32[]{:S(2)}, u32[]{:S(2)}) collective-permute-start(bf16[2,512,512]{2,1,0:T(8,128)(2,1)} %maximum_select_fusion.tok), channel_id=1, source_target_pairs={{0,1},{1,2},{2,3},{3,4},{4,5},{5,6},{6,7},{7,8},{8,9},{9,10},{10,1... | collective-permute-start | bytes 3145736 | tf_op jit(solution)/shard_map/ppermute | solution.py:866
  73.5 1.6 copy-done.12
  76.1 9.6 %attend_far.2 = (f32[2,512,256]{2,1,0:T(8,128)S(1)}, bf16[2,512,256]{2,1,0:T(8,128)(2,1)S(1)}, bf16[2,512,128]{2,1,0:T(8,128)(2,1)S(1)}, bf16[2,512,768]{2,1,0:T(8,128)(2,1)}, bf16[2,512,768]{2,1,0:T(8,128)(2,1)}) custom-call(s32[8]{0:T(128)S(1)} %squeeze.81.rng, f32[8,768]{1,0:T(8,128)S(1)} %broadcast_in_dim.170.bias, ...), custom_call_target="tpu_custom_call" | custom-call | flops 4000000000 | bytes 8000000 | tf_op jit(solution)/shard_map/attend_far/pallas_call | solution.py:484
  86.3 6.5 %attend_far.3 = (f32[2,512,256]{2,1,0:T(8,128)S(1)}, bf16[2,512,256]{2,1,0:T(8,128)(2,1)S(1)}, bf16[2,512,128]{2,1,0:T(8,128)(2,1)S(1)}, bf16[2,512,768]{2,1,0:T(8,128)(2,1)}, bf16[2,512,768]{2,1,0:T(8,128)(2,1)}) custom-call(s32[8]{0:T(128)S(1)} %squeeze.86.rng, f32[8,768]{1,0:T(8,128)S(1)} %broadcast_in_dim.170.bias, ...), custom_call_target="tpu_custom_call" | custom-call | flops 4000000000 | bytes 8000000 | tf_op jit(solution)/shard_map/attend_far/pallas_call | solution.py:484
  92.8 2.1 collective-permute-done.20.ctx_b.refs_12_
  94.9 11.5 %chain.2 = (bf16[512,512]{1,0:T(8,128)(2,1)S(1)}, f32[512,512]{1,0:T(8,128)}, bf16[512,256]{1,0:T(8,128)(2,1)S(1)}, bf16[512,256]{1,0:T(8,128)(2,1)S(1)}, bf16[5...) custom-call(bf16[2,1,512,512]{3,2,1,0:T(8,128)(2,1)S(1)} %copy-done., ...), custom_call_target="tpu_custom_call" | custom-call | flops 6000000000 | bytes 12000000 | tf_op jit(solution)/shard_map/chain/pallas_call | solution.py:655
  106.7 1.8 collective-permute-start.23
  108.6 4.2 %collective-permute-done.24 = bf16[512,256]{1,0:T(8,128)(2,1)S(1)} collective-permute-done((bf16[512,256]{1,0:T(8,128)(2,1)S(1)}, bf16[512,256]{1,0:T(8,128)(2,1)S(1)}, u32[]{:S(2)}, u32[]{:S(2)}) %collective-permute-start.24) | collective-permute-done | bytes 262176 | tf_op jit(solution)/shard_map/ppermute | solution.py:861
  112.9 1.8 payload.2
  115.6 11.5 %chain.3 = (bf16[512,512]{1,0:T(8,128)(2,1)S(1)}, f32[512,512]{1,0:T(8,128)}, bf16[512,256]{1,0:T(8,128)(2,1)S(1)}, bf16[512,256]{1,0:T(8,128)(2,1)S(1)}, bf16[5...) custom-call(bf16[2,1,512,512]{3,2,1,0:T(8,128)(2,1)S(1)} %copy-done., ...), custom_call_target="tpu_custom_call" | custom-call | flops 6000000000 | bytes 12000000 | tf_op jit(solution)/shard_map/chain/pallas_call | solution.py:655
  127.1 1.3 collective-permute-start.27
  128.4 21.8 %collective-permute-start.26 = (bf16[2,512,384]{2,1,0:T(8,128)(2,1)}, bf16[2,512,384]{2,1,0:T(8,128)(2,1)}, u32[]{:S(2)}, u32[]{:S(2)}) collective-permute-start(bf16[2,512,384]{2,1,0:T(8,128)(2,1)} %payload.2), channel_id=1, source_target_pairs={{0,1},{1,2},{2,3},{3,4},{4,5},{5,6},{6,7},{7,8},{8,9},{9,10},{10,1... | collective-permute-start | bytes 2359304 | tf_op jit(solution)/shard_map/ppermute | solution.py:866
  150.2 1.4 collective-permute-start.25
  151.7 8.7 %weight_grads.1 = bf16[4624,512]{1,0:T(8,128)(2,1)} custom-call(bf16[512,2048]{1,0:T(8,128)(2,1)S(1)} %get-tuple-element.197.refs_0_, bf16[512,2048]{1,0:T(8,128)(2,1)S(1)} %get-tuple-element.198.refs_1_, bf16[512,512]{1,0:T(8,128)(2,1)S(1)} %get-tuple-element.199.refs_2_, bf16[512,512]{1,0:T(8,128)(2,1)S(1)} %get-tuple-element.200.refs_3_, ...), custom_call_target="tpu_custom_call" | custom-call | flops 1000000000 | bytes 2000000 | tf_op jit(solution)/shard_map/weight_grads/pallas_call | solution.py:736
  162.8 1.9 payload.3
  164.6 131.1 %conditional.1 = (f32[2,1,512,512]{3,2,1,0:T(8,128)}, f32[512,1536]{1,0:T(8,128)}, f32[16,1024]{1,0:T(8,128)}, f32[1,512]{1,0:T(1,128)}, f32[1,512]{1,0:T(1,128)}, /*index=5*/f32[512]{0:T(512)S(1)}, f32[512]{0:T(512)S(1)}) conditional(s32[]{:T(128)} %bitcast.72, () %tuple.27, (s32[]{:T(128)}, s32[]{:T(128)}, s32[2,4,2]{1,0,2:T(2,128)S(1)}, ...), branch_computations={%region_6.7_spmd, %region_7.8_spmd} | conditional | flops 51318296576 | bytes 140407264 | solution.py:1117
  164.6 1.3 collective-permute-start.1
  165.9 6.5 %collective-permute-start = (bf16[2,512,384]{2,1,0:T(8,128)(2,1)}, bf16[2,512,384]{2,1,0:T(8,128)(2,1)}, u32[]{:S(2)}, u32[]{:S(2)}) collective-permute-start(bf16[2,512,384]{2,1,0:T(8,128)(2,1)} %get-tuple-element.58.rest_1_), channel_id=1, source_target_pairs={{0,1},{1,2},{2,3},{3,4},{4,5},{5,6},{6,7},{7,8},{8,9},{9,10},{10,1... | collective-permute-start | bytes 2359304 | tf_op jit(solution)/shard_map/cond/branch_1_fun/ppermute | solution.py:866
  172.6 1.3 slice_bitcast_fusion.2
  174.3 1.2 copy-done.38
  176.0 18.8 %attend_back.2.refs_2_ = bf16[2,512,768]{2,1,0:T(8,128)(2,1)S(1)} custom-call(s32[8]{0:T(128)S(1)} %squeeze.29.rng, bf16[1536,128]{1,0:T(8,128)(2,1)S(1)} %get-tuple-element.388.fq, bf16[2,1536,128]{2,1,0:T(8,128)(2,1)S(1)} %get-tuple-element.384.fk, bf16[2,512,384]{2,1,0:T(8,128)(2,1)} %get-tuple-element.52.rest_0_, ...), custom_call_target="tpu_custom_call" | custom-call | flops 24000000000 | bytes 12000000 | tf_op jit(solution)/shard_map/cond/branch_1_fun/attend_back/pallas_call | solution.py:502
  194.8 2.5 convolution_convert_fusion.1
  198.0 20.5 %attend_back.3.refs_3_ = bf16[2,512,768]{2,1,0:T(8,128)(2,1)S(1)} custom-call(s32[8]{0:T(128)S(1)} %squeeze.62.rng, bf16[1536,128]{1,0:T(8,128)(2,1)S(1)} %get-tuple-element.387.fq, bf16[2,1536,128]{2,1,0:T(8,128)(2,1)S(1)} %get-tuple-element.383.fk, bf16[2,512,384]{2,1,0:T(8,128)(2,1)} %collective-permute-done.rest_0_, ...), custom_call_target="tpu_custom_call" | custom-call | flops 24000000000 | bytes 12000000 | tf_op jit(solution)/shard_map/cond/branch_1_fun/attend_back/pallas_call | solution.py:502
  218.6 4.5 %qkv_weight_grad.1 = bf16[640,768]{1,0:T(8,128)(2,1)S(1)} custom-call(bf16[2,512,512]{2,1,0:T(8,128)(2,1)} %get-tuple-element.47.refs_0_, bf16[2,512,512]{2,1,0:T(8,128)(2,1)} %get-tuple-element.48.refs_1_, bf16[2,512,768]{2,1,0:T(8,128)(2,1)S(1)} %attend_back.2.refs_2_, bf16[2,512,768]{2,1,0:T(8,128)(2,1)S(1)} %attend_back.3.refs_3_, ...), custom_call_target="tpu_custom_call" | custom-call | flops 1600000000 | bytes 4000000 | tf_op jit(solution)/shard_map/cond/branch_1_fun/qkv_weight_grad/pallas_call | solution.py:807
  223.9 9.5 %collective-permute-start.3 = (bf16[8,40,768]{2,1,0:T(8,128)(2,1)}, bf16[8,40,768]{2,1,0:T(8,128)(2,1)}, u32[]{:S(2)}, u32[]{:S(2)}) collective-permute-start(bf16[8,40,768]{2,1,0:T(8,128)(2,1)} %dynamic-slice_bitcast_fusion), channel_id=1, source_target_pairs={{0,1},{1,0},{2,3},{3,2},{4,5},{5,4},{6,7},{7,6},{8,9},{9,8},{10,11... | collective-permute-start | bytes 1474568 | tf_op jit(solution)/shard_map/cond/branch_1_fun/ppermute | solution.py:904
  233.5 1.8 collective-permute-done.3
  235.3 1.1 fusion
  236.6 1.8 convolution_convert_fusion
  238.4 1.5 collective-permute-start.8
  239.9 4.9 %collective-permute-done.4 = bf16[4,40,768]{2,1,0:T(8,128)(2,1)S(1)} collective-permute-done((bf16[4,40,768]{2,1,0:T(8,128)(2,1)S(1)}, bf16[4,40,768]{2,1,0:T(8,128)(2,1)S(1)}, u32[]{:S(2)}, u32[]{:S(2)}) %collective-permute-start.4) | collective-permute-done | bytes 245792 | tf_op jit(solution)/shard_map/cond/branch_1_fun/ppermute | solution.py:904
  245.0 3.8 %collective-permute-start.7 = (bf16[1,40,768]{2,1,0:T(8,128)(2,1)S(1)}, bf16[1,40,768]{2,1,0:T(8,128)(2,1)S(1)}, u32[]{:S(2)}, u32[]{:S(2)}) collective-permute-start(bf16[1,40,768]{2,1,0:T(8,128)(2,1)S(1)} %get-tuple-element.398), channel_id=1, source_target_pairs={{0,12},{1,13},{2,14},{3,15},{4,8},{5,9},{6,10},{7,11},{8,4},{9,5},... | collective-permute-start | bytes 184328 | tf_op jit(solution)/shard_map/cond/branch_1_fun/ppermute | solution.py:904
  249.4 2.9 collective-permute-done.7
  252.3 2.8 collective-permute-done.6
  256.0 2.6 collective-permute-start.10
  258.6 1.7 collective-permute-start.9
  261.5 2.4 collective-permute-done.10
  266.5 1.3 collective-permute-start.14
  268.8 1.2 collective-permute-start.12
  270.0 8.3 %collective-permute-done.14 = bf16[4,40,768]{2,1,0:T(8,128)(2,1)} collective-permute-done((bf16[4,40,768]{2,1,0:T(8,128)(2,1)}, bf16[4,40,768]{2,1,0:T(8,128)(2,1)}, u32[]{:S(2)}, u32[]{:S(2)}) %collective-permute-start.14) | collective-permute-done | bytes 245792 | tf_op jit(solution)/shard_map/cond/branch_1_fun/ppermute | solution.py:904
  279.5 3.0 collective-permute-done.12
  282.5 1.1 select_bitcast_fusion.5
  284.8 2.0 convolution_add_fusion.refs_0_
  287.7 1.6 select_bitcast_fusion.1
  290.4 2.7 finish.1
  293.1 1.3 fusion.23
  295.8 24.5 %all-reduce.2.cloned.1.call-done.cells = bf16[4624,512]{1,0:T(8,128)(2,1)} async-done(((bf16[4624,512]{1,0:T(8,128)(2,1)}), bf16[4624,512]{1,0:T(8,128)(2,1)}) %all-reduce.2.cloned.1.call-update) | async-done | bytes 4734992 | tf_op jit(solution)/shard_map/psum | solution.py:1105
  322.2 2.3 copy-done
  324.6 5.9 %unpack.1 = (f32[2048,512]{1,0:T(8,128)}, f32[512,2048]{1,0:T(8,128)}, f32[512,512]{1,0:T(8,128)}) custom-call(bf16[4624,512]{1,0:T(8,128)(2,1)S(1)} %copy-done), custom_call_target="tpu_custom_call" | custom-call | flops 100000000 | bytes 16000000 | tf_op jit(solution)/shard_map/unpack/pallas_call | solution.py:768
  (181 shorter events, 28.4 us)
Async XLA Ops:
  7.2 5.5 %copy-start.36 = (bf16[512]{0:T(512)(128)(2,1)S(1)}, bf16[512]{0:T(512)(128)(2,1)}, u32[]{:S(2)}) copy-start(bf16[512]{0:T(512)(128)(2,1)} %param.21) | copy-start | bytes 3076
  7.2 5.5 %copy-start.37 = (bf16[512]{0:T(512)(128)(2,1)S(1)}, bf16[512]{0:T(512)(128)(2,1)}, u32[]{:S(2)}) copy-start(bf16[512]{0:T(512)(128)(2,1)} %param.22) | copy-start | bytes 3076
  7.2 5.5 %copy-start.29 = (s32[2,2,96]{2,1,0:T(2,128)S(1)}, s32[2,2,96]{2,1,0:T(2,128)}, u32[]{:S(2)}) copy-start(s32[2,2,96]{2,1,0:T(2,128)} %param.19) | copy-start | bytes 4612
  7.2 13.8 %copy-start.23 = (bf16[512,1536]{1,0:T(8,128)(2,1)S(1)}, bf16[512,1536]{1,0:T(8,128)(2,1)}, u32[]{:S(2)}) copy-start(bf16[512,1536]{1,0:T(8,128)(2,1)} %param.20) | copy-start | bytes 4718596
  7.2 313.1 %all-reduce.2.cloned.1.call-start = ((), (), s32[]{:S(2)}) async-start(), calls=%async_computation | async-start | bytes 9469952 | tf_op jit(solution)/shard_map/psum | solution.py:1105
  9.7 15.2 %collective-permute-start.16 = (bf16[512,512]{1,0:T(8,128)(2,1)}, bf16[512,512]{1,0:T(8,128)(2,1)}, u32[]{:S(2)}, u32[]{:S(2)}) collective-permute-start(bf16[512,512]{1,0:T(8,128)(2,1)} %get-tuple-element.407), channel_id=1, source_target_pairs={{0,16},{16,0},{1,17},{17,1},{2,18},{18,2},{3,19},{19,3},{4,20},{20... | collective-permute-start | bytes 1572872 | tf_op jit(solution)/shard_map/ppermute | solution.py:861
  23.7 1.2 copy-start.17
  24.9 7.8 %copy-start.21 = (bf16[512,1536]{0,1:T(8,128)(2,1)S(1)}, bf16[512,1536]{0,1:T(8,128)(2,1)}, u32[]{:S(2)}) copy-start(bf16[512,1536]{0,1:T(8,128)(2,1)} %copy.92) | copy-start | bytes 4718596
  27.4 39.5 %collective-permute-start.19 = (bf16[2,512,512]{2,1,0:T(8,128)(2,1)}, bf16[2,512,512]{2,1,0:T(8,128)(2,1)}, u32[]{:S(2)}, u32[]{:S(2)}) collective-permute-start(bf16[2,512,512]{2,1,0:T(8,128)(2,1)} %maximum_select_fusion.1.tok), channel_id=1, source_target_pairs={{1,0},{2,1},{3,2},{4,3},{5,4},{6,5},{7,6},{8,7},{9,8},{10,9},{11,1... | collective-permute-start | bytes 3145736 | tf_op jit(solution)/shard_map/ppermute | solution.py:866
  28.7 38.2 %collective-permute-start.18 = (bf16[2,512,512]{2,1,0:T(8,128)(2,1)}, bf16[2,512,512]{2,1,0:T(8,128)(2,1)}, u32[]{:S(2)}, u32[]{:S(2)}) collective-permute-start(bf16[2,512,512]{2,1,0:T(8,128)(2,1)} %maximum_select_fusion.1.tok), channel_id=1, source_target_pairs={{0,1},{1,2},{2,3},{3,4},{4,5},{5,6},{6,7},{7,8},{8,9},{9,10},{10,1... | collective-permute-start | bytes 3145736 | tf_op jit(solution)/shard_map/ppermute | solution.py:866
  33.6 15.3 %collective-permute-start.17 = (bf16[512,512]{1,0:T(8,128)(2,1)}, bf16[512,512]{1,0:T(8,128)(2,1)S(1)}, u32[]{:S(2)}, u32[]{:S(2)}) collective-permute-start(bf16[512,512]{1,0:T(8,128)(2,1)} %get-tuple-element.160), channel_id=1, source_target_pairs={{0,16},{16,0},{1,17},{17,1},{2,18},{18,2},{3,19},{19,3},{4,20},{20... | collective-permute-start | bytes 1572872 | tf_op jit(solution)/shard_map/ppermute | solution.py:861
  36.4 12.6 %copy-start.22 = (bf16[512,512]{1,0:T(8,128)(2,1)S(1)}, bf16[512,512]{1,0:T(8,128)(2,1)}, u32[]{:S(2)}) copy-start(bf16[512,512]{1,0:T(8,128)(2,1)} %get-tuple-element.160) | copy-start | bytes 1572868
  49.0 1.7 copy-start.11
  50.6 21.6 %copy-start.30 = (bf16[512]{0:T(512)(128)(2,1)S(1)}, bf16[512]{0:T(512)(128)(2,1)}, u32[]{:S(2)}) copy-start(bf16[512]{0:T(512)(128)(2,1)} %param.24) | copy-start | bytes 3076
  50.6 21.6 %copy-start.31 = (bf16[512]{0:T(512)(128)(2,1)S(1)}, bf16[512]{0:T(512)(128)(2,1)}, u32[]{:S(2)}) copy-start(bf16[512]{0:T(512)(128)(2,1)} %param.25) | copy-start | bytes 3076
  50.6 21.6 %copy-start.32 = (bf16[512]{0:T(512)(128)(2,1)S(1)}, bf16[512]{0:T(512)(128)(2,1)}, u32[]{:S(2)}) copy-start(bf16[512]{0:T(512)(128)(2,1)} %param.26) | copy-start | bytes 3076
  50.6 21.6 %copy-start.33 = (bf16[512]{0:T(512)(128)(2,1)S(1)}, bf16[512]{0:T(512)(128)(2,1)}, u32[]{:S(2)}) copy-start(bf16[512]{0:T(512)(128)(2,1)} %param.30) | copy-start | bytes 3076
  50.6 21.7 %copy-start.34 = (bf16[512]{0:T(512)(128)(2,1)S(1)}, bf16[512]{0:T(512)(128)(2,1)}, u32[]{:S(2)}) copy-start(bf16[512]{0:T(512)(128)(2,1)} %param.31) | copy-start | bytes 3076
  50.6 21.7 %copy-start.35 = (bf16[512]{0:T(512)(128)(2,1)S(1)}, bf16[512]{0:T(512)(128)(2,1)}, u32[]{:S(2)}) copy-start(bf16[512]{0:T(512)(128)(2,1)} %param.32) | copy-start | bytes 3076
  50.6 21.7 %copy-start.26 = (bf16[2048]{0:T(1024)(128)(2,1)S(1)}, bf16[2048]{0:T(1024)(128)(2,1)}, u32[]{:S(2)}) copy-start(bf16[2048]{0:T(1024)(128)(2,1)} %param.28) | copy-start | bytes 12292
  64.8 1.3 copy-start.9
  66.9 19.4 %collective-permute-start.22 = (bf16[2,512,512]{2,1,0:T(8,128)(2,1)}, bf16[2,512,512]{2,1,0:T(8,128)(2,1)}, u32[]{:S(2)}, u32[]{:S(2)}) collective-permute-start(bf16[2,512,512]{2,1,0:T(8,128)(2,1)} %maximum_select_fusion.tok), channel_id=1, source_target_pairs={{1,0},{2,1},{3,2},{4,3},{5,4},{6,5},{7,6},{8,7},{9,8},{10,9},{11,1... | collective-permute-start | bytes 3145736 | tf_op jit(solution)/shard_map/ppermute | solution.py:866
  68.2 18.1 %collective-permute-start.21 = (bf16[2,512,512]{2,1,0:T(8,128)(2,1)}, bf16[2,512,512]{2,1,0:T(8,128)(2,1)}, u32[]{:S(2)}, u32[]{:S(2)}) collective-permute-start(bf16[2,512,512]{2,1,0:T(8,128)(2,1)} %maximum_select_fusion.tok), channel_id=1, source_target_pairs={{0,1},{1,2},{2,3},{3,4},{4,5},{5,6},{6,7},{7,8},{8,9},{9,10},{10,1... | collective-permute-start | bytes 3145736 | tf_op jit(solution)/shard_map/ppermute | solution.py:866
  73.5 1.6 copy-start.12
  76.1 10.2 %copy-start.10 = (f32[4,4,256,128]{3,2,1,0:T(8,128)S(1)}, f32[4,4,256,128]{3,2,1,0:T(8,128)}, u32[]{:S(2)}) copy-start(f32[4,4,256,128]{3,2,1,0:T(8,128)} %copy-done.9) | copy-start | bytes 6291460
  76.1 10.2 %copy-start.14 = (f32[4,256,128]{2,1,0:T(8,128)S(1)}, f32[4,256,128]{2,1,0:T(8,128)}, u32[]{:S(2)}) copy-start(f32[4,256,128]{2,1,0:T(8,128)} %copy-done.13) | copy-start | bytes 1572868
  76.1 10.2 %copy-start.39 = (bf16[2,512,768]{2,1,0:T(8,128)(2,1)S(1)}, bf16[2,512,768]{2,1,0:T(8,128)(2,1)}, u32[]{:S(2)}) copy-start(bf16[2,512,768]{2,1,0:T(8,128)(2,1)} %get-tuple-element.179.lin) | copy-start | bytes 4718596
  85.7 9.1 %copy-start.3 = (bf16[2,1,512,512]{3,2,1,0:T(8,128)(2,1)S(1)}, bf16[2,1,512,512]{3,2,1,0:T(8,128)(2,1)}, u32[]{:S(2)}) copy-start(bf16[2,1,512,512]{3,2,1,0:T(8,128)(2,1)} %tok.3) | copy-start | bytes 3145732
  85.7 9.1 %copy-start.6 = (bf16[512,2048]{1,0:T(8,128)(2,1)S(1)}, bf16[512,2048]{1,0:T(8,128)(2,1)}, u32[]{:S(2)}) copy-start(bf16[512,2048]{1,0:T(8,128)(2,1)} %up.3) | copy-start | bytes 6291460
  85.8 9.1 %copy-start.7 = (bf16[2048,512]{1,0:T(8,128)(2,1)S(1)}, bf16[2048,512]{1,0:T(8,128)(2,1)}, u32[]{:S(2)}) copy-start(bf16[2048,512]{1,0:T(8,128)(2,1)} %down.3) | copy-start | bytes 6291460
  85.8 9.1 %copy-start.8 = (bf16[2,1,512,512]{3,2,1,0:T(8,128)(2,1)S(1)}, bf16[2,1,512,512]{3,2,1,0:T(8,128)(2,1)}, u32[]{:S(2)}) copy-start(bf16[2,1,512,512]{3,2,1,0:T(8,128)(2,1)} %cot.3) | copy-start | bytes 3145732
  85.8 9.1 %collective-permute-start.20 = (bf16[512,256]{1,0:T(8,128)(2,1)S(1)}, bf16[512,256]{1,0:T(8,128)(2,1)S(1)}, u32[]{:S(2)}, u32[]{:S(2)}) collective-permute-start(bf16[512,256]{1,0:T(8,128)(2,1)S(1)} %get-tuple-element.411), channel_id=1, source_target_pairs={{0,16},{16,0},{1,17},{17,1},{2,18},{18,2},{3,19},{19,3},{4,20},{20... | collective-permute-start | bytes 786440 | tf_op jit(solution)/shard_map/ppermute | solution.py:861
  106.4 6.4 %collective-permute-start.24 = (bf16[512,256]{1,0:T(8,128)(2,1)S(1)}, bf16[512,256]{1,0:T(8,128)(2,1)S(1)}, u32[]{:S(2)}, u32[]{:S(2)}) collective-permute-start(bf16[512,256]{1,0:T(8,128)(2,1)S(1)} %get-tuple-element.194), channel_id=1, source_target_pairs={{0,16},{16,0},{1,17},{17,1},{2,18},{18,2},{3,19},{19,3},{4,20},{20... | collective-permute-start | bytes 786440 | tf_op jit(solution)/shard_map/ppermute | solution.py:861
  106.7 8.9 %collective-permute-start.23 = (bf16[512,256]{1,0:T(8,128)(2,1)S(1)}, bf16[512,256]{1,0:T(8,128)(2,1)S(1)}, u32[]{:S(2)}, u32[]{:S(2)}) collective-permute-start(bf16[512,256]{1,0:T(8,128)(2,1)S(1)} %get-tuple-element.415), channel_id=1, source_target_pairs={{0,16},{16,0},{1,17},{17,1},{2,18},{18,2},{3,19},{19,3},{4,20},{20... | collective-permute-start | bytes 786440 | tf_op jit(solution)/shard_map/ppermute | solution.py:861
  127.1 33.3 %collective-permute-start.27 = (bf16[2,512,384]{2,1,0:T(8,128)(2,1)}, bf16[2,512,384]{2,1,0:T(8,128)(2,1)}, u32[]{:S(2)}, u32[]{:S(2)}) collective-permute-start(bf16[2,512,384]{2,1,0:T(8,128)(2,1)} %payload.2), channel_id=1, source_target_pairs={{1,0},{2,1},{3,2},{4,3},{5,4},{6,5},{7,6},{8,7},{9,8},{10,9},{11,1... | collective-permute-start | bytes 2359304 | tf_op jit(solution)/shard_map/ppermute | solution.py:866
  128.4 32.0 %collective-permute-start.26 = (bf16[2,512,384]{2,1,0:T(8,128)(2,1)}, bf16[2,512,384]{2,1,0:T(8,128)(2,1)}, u32[]{:S(2)}, u32[]{:S(2)}) collective-permute-start(bf16[2,512,384]{2,1,0:T(8,128)(2,1)} %payload.2), channel_id=1, source_target_pairs={{0,1},{1,2},{2,3},{3,4},{4,5},{5,6},{6,7},{7,8},{8,9},{9,10},{10,1... | collective-permute-start | bytes 2359304 | tf_op jit(solution)/shard_map/ppermute | solution.py:866
  150.2 10.2 %collective-permute-start.25 = (bf16[512,256]{1,0:T(8,128)(2,1)S(1)}, bf16[512,256]{1,0:T(8,128)(2,1)S(1)}, u32[]{:S(2)}, u32[]{:S(2)}) collective-permute-start(bf16[512,256]{1,0:T(8,128)(2,1)S(1)} %get-tuple-element.211), channel_id=1, source_target_pairs={{0,16},{16,0},{1,17},{17,1},{2,18},{18,2},{3,19},{19,3},{4,20},{20... | collective-permute-start | bytes 786440 | tf_op jit(solution)/shard_map/ppermute | solution.py:861
  162.8 1.9 copy-start.18
  164.6 33.4 %collective-permute-start.1 = (bf16[2,512,384]{2,1,0:T(8,128)(2,1)}, bf16[2,512,384]{2,1,0:T(8,128)(2,1)}, u32[]{:S(2)}, u32[]{:S(2)}) collective-permute-start(bf16[2,512,384]{2,1,0:T(8,128)(2,1)} %get-tuple-element.58.rest_1_), channel_id=1, source_target_pairs={{1,0},{2,1},{3,2},{4,3},{5,4},{6,5},{7,6},{8,7},{9,8},{10,9},{11,1... | collective-permute-start | bytes 2359304 | tf_op jit(solution)/shard_map/cond/branch_1_fun/ppermute | solution.py:866
  165.9 32.1 %collective-permute-start = (bf16[2,512,384]{2,1,0:T(8,128)(2,1)}, bf16[2,512,384]{2,1,0:T(8,128)(2,1)}, u32[]{:S(2)}, u32[]{:S(2)}) collective-permute-start(bf16[2,512,384]{2,1,0:T(8,128)(2,1)} %get-tuple-element.58.rest_1_), channel_id=1, source_target_pairs={{0,1},{1,2},{2,3},{3,4},{4,5},{5,6},{6,7},{7,8},{8,9},{9,10},{10,1... | collective-permute-start | bytes 2359304 | tf_op jit(solution)/shard_map/cond/branch_1_fun/ppermute | solution.py:866
  172.6 1.7 copy-start.41
  173.9 1.6 copy-start.38
  174.0 2.0 copy-start.40
  197.3 21.3 %collective-permute-start.2 = (bf16[512,512]{1,0:T(8,128)(2,1)}, bf16[512,512]{1,0:T(8,128)(2,1)S(1)}, u32[]{:S(2)}, u32[]{:S(2)}) collective-permute-start(bf16[512,512]{1,0:T(8,128)(2,1)} %convolution_convert_fusion.1), channel_id=1, source_target_pairs={{0,16},{16,0},{1,17},{17,1},{2,18},{18,2},{3,19},{19,3},{4,20},{20... | collective-permute-start | bytes 1572872 | tf_op jit(solution)/shard_map/cond/branch_1_fun/ppermute | solution.py:861
  218.5 4.6 %copy-start.1 = (bf16[2,512,768]{2,1,0:T(8,128)(2,1)}, bf16[2,512,768]{2,1,0:T(8,128)(2,1)S(1)}, u32[]{:S(2)}) copy-start(bf16[2,512,768]{2,1,0:T(8,128)(2,1)S(1)} %attend_back.3.refs_3_) | copy-start | bytes 4718596 | tf_op jit(solution)/shard_map/cond
  223.9 11.4 %collective-permute-start.3 = (bf16[8,40,768]{2,1,0:T(8,128)(2,1)}, bf16[8,40,768]{2,1,0:T(8,128)(2,1)}, u32[]{:S(2)}, u32[]{:S(2)}) collective-permute-start(bf16[8,40,768]{2,1,0:T(8,128)(2,1)} %dynamic-slice_bitcast_fusion), channel_id=1, source_target_pairs={{0,1},{1,0},{2,3},{3,2},{4,5},{5,4},{6,7},{7,6},{8,9},{9,8},{10,11... | collective-permute-start | bytes 1474568 | tf_op jit(solution)/shard_map/cond/branch_1_fun/ppermute | solution.py:904
  233.5 3.1 copy-start.2
  236.5 12.3 %copy-start.20 = (bf16[512,768]{0,1:T(8,128)(2,1)S(1)}, bf16[512,768]{0,1:T(8,128)(2,1)}, u32[]{:S(2)}) copy-start(bf16[512,768]{0,1:T(8,128)(2,1)} %get-tuple-element.354) | copy-start | bytes 2359300 | tf_op jit(solution)/shard_map/cond
  236.5 12.3 %copy-start.24 = (f32[512,512]{1,0:T(8,128)S(1)}, f32[512,512]{1,0:T(8,128)}, u32[]{:S(2)}) copy-start(f32[512,512]{1,0:T(8,128)} %get-tuple-element.63) | copy-start | bytes 3145732 | tf_op jit(solution)/shard_map/cond
  236.5 8.3 %collective-permute-start.4 = (bf16[4,40,768]{2,1,0:T(8,128)(2,1)S(1)}, bf16[4,40,768]{2,1,0:T(8,128)(2,1)S(1)}, u32[]{:S(2)}, u32[]{:S(2)}) collective-permute-start(bf16[4,40,768]{2,1,0:T(8,128)(2,1)S(1)} %dynamic-slice_bitcast_fusion.1), channel_id=1, source_target_pairs={{0,2},{1,3},{2,0},{3,1},{4,6},{5,7},{6,4},{7,5},{8,10},{9,11},{10,... | collective-permute-start | bytes 737288 | tf_op jit(solution)/shard_map/cond/branch_1_fun/ppermute | solution.py:904
  238.4 16.8 %collective-permute-start.8 = (bf16[512,512]{1,0:T(8,128)(2,1)S(1)}, bf16[512,512]{1,0:T(8,128)(2,1)S(1)}, u32[]{:S(2)}, u32[]{:S(2)}) collective-permute-start(bf16[512,512]{1,0:T(8,128)(2,1)S(1)} %convolution_convert_fusion), channel_id=1, source_target_pairs={{0,16},{16,0},{1,17},{17,1},{2,18},{18,2},{3,19},{19,3},{4,20},{20... | collective-permute-start | bytes 1572872 | tf_op jit(solution)/shard_map/cond/branch_1_fun/ppermute | solution.py:861
  244.9 4.5 %collective-permute-start.5 = (bf16[1,40,768]{2,1,0:T(8,128)(2,1)S(1)}, bf16[1,40,768]{2,1,0:T(8,128)(2,1)S(1)}, u32[]{:S(2)}, u32[]{:S(2)}) collective-permute-start(bf16[1,40,768]{2,1,0:T(8,128)(2,1)S(1)} %get-tuple-element.397), channel_id=1, source_target_pairs={{0,4},{1,5},{2,6},{3,7},{4,0},{5,1},{6,2},{7,3},{8,12},{9,13},{10,... | collective-permute-start | bytes 184328 | tf_op jit(solution)/shard_map/cond/branch_1_fun/ppermute | solution.py:904
  245.0 7.3 %collective-permute-start.7 = (bf16[1,40,768]{2,1,0:T(8,128)(2,1)S(1)}, bf16[1,40,768]{2,1,0:T(8,128)(2,1)S(1)}, u32[]{:S(2)}, u32[]{:S(2)}) collective-permute-start(bf16[1,40,768]{2,1,0:T(8,128)(2,1)S(1)} %get-tuple-element.398), channel_id=1, source_target_pairs={{0,12},{1,13},{2,14},{3,15},{4,8},{5,9},{6,10},{7,11},{8,4},{9,5},... | collective-permute-start | bytes 184328 | tf_op jit(solution)/shard_map/cond/branch_1_fun/ppermute | solution.py:904
  248.8 6.3 %collective-permute-start.6 = (bf16[1,40,768]{2,1,0:T(8,128)(2,1)S(1)}, bf16[1,40,768]{2,1,0:T(8,128)(2,1)S(1)}, u32[]{:S(2)}, u32[]{:S(2)}) collective-permute-start(bf16[1,40,768]{2,1,0:T(8,128)(2,1)S(1)} %get-tuple-element.399), channel_id=1, source_target_pairs={{0,8},{1,9},{2,10},{3,11},{4,12},{5,13},{6,14},{7,15},{8,0},{9,1},... | collective-permute-start | bytes 184328 | tf_op jit(solution)/shard_map/cond/branch_1_fun/ppermute | solution.py:904
  256.0 5.5 %collective-permute-start.11 = (bf16[1,40,768]{2,1,0:T(8,128)(2,1)S(1)}, bf16[1,40,768]{2,1,0:T(8,128)(2,1)S(1)}, u32[]{:S(2)}, u32[]{:S(2)}) collective-permute-start(bf16[1,40,768]{2,1,0:T(8,128)(2,1)S(1)} %add_convert_fusion), channel_id=1, source_target_pairs={{0,4},{1,5},{2,6},{3,7},{4,0},{5,1},{6,2},{7,3},{8,12},{9,13},{10,... | collective-permute-start | bytes 184328 | tf_op jit(solution)/shard_map/cond/branch_1_fun/ppermute | solution.py:904
  256.0 7.9 %collective-permute-start.10 = (bf16[1,40,768]{2,1,0:T(8,128)(2,1)S(1)}, bf16[1,40,768]{2,1,0:T(8,128)(2,1)S(1)}, u32[]{:S(2)}, u32[]{:S(2)}) collective-permute-start(bf16[1,40,768]{2,1,0:T(8,128)(2,1)S(1)} %add_convert_fusion), channel_id=1, source_target_pairs={{0,8},{1,9},{2,10},{3,11},{4,12},{5,13},{6,14},{7,15},{8,0},{9,1},... | collective-permute-start | bytes 184328 | tf_op jit(solution)/shard_map/cond/branch_1_fun/ppermute | solution.py:904
  258.6 6.2 %collective-permute-start.9 = (bf16[1,40,768]{2,1,0:T(8,128)(2,1)S(1)}, bf16[1,40,768]{2,1,0:T(8,128)(2,1)}, u32[]{:S(2)}, u32[]{:S(2)}) collective-permute-start(bf16[1,40,768]{2,1,0:T(8,128)(2,1)S(1)} %add_convert_fusion), channel_id=1, source_target_pairs={{0,12},{1,13},{2,14},{3,15},{4,8},{5,9},{6,10},{7,11},{8,4},{9,5},... | collective-permute-start | bytes 184328 | tf_op jit(solution)/shard_map/cond/branch_1_fun/ppermute | solution.py:904
  266.5 11.8 %collective-permute-start.14 = (bf16[4,40,768]{2,1,0:T(8,128)(2,1)}, bf16[4,40,768]{2,1,0:T(8,128)(2,1)}, u32[]{:S(2)}, u32[]{:S(2)}) collective-permute-start(bf16[4,40,768]{2,1,0:T(8,128)(2,1)} %maximum_bitcast_fusion), channel_id=1, source_target_pairs={{0,2},{1,3},{2,0},{3,1},{4,6},{5,7},{6,4},{7,5},{8,10},{9,11},{10,... | collective-permute-start | bytes 737288 | tf_op jit(solution)/shard_map/cond/branch_1_fun/ppermute | solution.py:904
  267.8 11.7 %collective-permute-start.13 = (bf16[4,40,768]{2,1,0:T(8,128)(2,1)}, bf16[4,40,768]{2,1,0:T(8,128)(2,1)}, u32[]{:S(2)}, u32[]{:S(2)}) collective-permute-start(bf16[4,40,768]{2,1,0:T(8,128)(2,1)} %maximum_bitcast_fusion), channel_id=1, source_target_pairs={{0,16},{1,17},{2,18},{3,19},{4,20},{5,21},{6,22},{7,23},{8,24},{9,... | collective-permute-start | bytes 737288 | tf_op jit(solution)/shard_map/cond/branch_1_fun/ppermute | solution.py:904
  268.8 13.7 %collective-permute-start.12 = (bf16[4,40,768]{2,1,0:T(8,128)(2,1)}, bf16[4,40,768]{2,1,0:T(8,128)(2,1)}, u32[]{:S(2)}, u32[]{:S(2)}) collective-permute-start(bf16[4,40,768]{2,1,0:T(8,128)(2,1)} %maximum_bitcast_fusion), channel_id=1, source_target_pairs={{0,18},{1,19},{2,16},{3,17},{4,22},{5,23},{6,20},{7,21},{8,26},{9,... | collective-permute-start | bytes 737288 | tf_op jit(solution)/shard_map/cond/branch_1_fun/ppermute | solution.py:904
  284.8 2.9 collective-permute-start.15
  295.8 34.7 %copy-start.27 = (f32[512]{0:T(512)}, f32[512]{0:T(512)S(1)}, u32[]{:S(2)}) copy-start(f32[512]{0:T(512)S(1)} %get-tuple-element.363) | copy-start | bytes 6148
  295.8 34.7 %copy-start.28 = (f32[512]{0:T(512)}, f32[512]{0:T(512)S(1)}, u32[]{:S(2)}) copy-start(f32[512]{0:T(512)S(1)} %get-tuple-element.362) | copy-start | bytes 6148
  322.2 2.3 copy-start
  (7 other events, 6.0 us)
Sparse Core Ops, SparseCore 0:
  160.6 159.6 all-reduce.1

commit v2 on v1

--- a/solution.py
+++ b/solution.py
@@ -203,13 +203,13 @@
     lane = lanes_of(rows)
 
     def per_tile(tile, carry):
-        make_queries(qa, lin, slot_start(tile), query_codes(fq, slot_start(tile + tiles)))
+        make_queries(qa, lin, slot_start(tile), query_codes(fq, slot_start(tile)))
         for head in range(GROUP):
             peak[head] = jnp.full((rows, LANES), FLOOR_MAX, F32)
             acc[head] = jnp.zeros((rows, LANES), F32)
 
         def step(other, inner):
-            code = both(fk, slot_start(other + tiles), slice(0, LANES))
+            code = both(fk, slot_start(other), slice(0, LANES))
             attend_step(qa, peak, acc, lin, slot_start(other), code)
             return inner
 
@@ -227,20 +227,32 @@
 
 
 def far_kernel(
-    tiles, rng, bias, fq, fk, weights, before, after, lin, acc_in, peak_in,
-    ctx_out, ctx_r_out, stat_out, lin_before, lin_after, qa, peak, acc,
+    tiles, rng, bias, fq, fk_before, fk_after, weights, before, after, lin, acc_in, peak_in,
+    ctx_out, ctx_r_out, stat_out, before_out, after_out, qa, peak, acc, lin_before, lin_after, sems,
 ):
     rows = 2 * SLOT_TILE
     lane = lanes_of(rows)
-    lax.fori_loop(
-        jnp.minimum(rng[0], tiles), tiles, projector(before, lin_before, weights, bias), 0
+    reach = (
+        (before, lin_before, before_out, jnp.minimum(rng[0], tiles), tiles, 0),
+        (after, lin_after, after_out, 0, jnp.maximum(rng[2 * tiles - 1] - 2 * tiles, 0), tiles),
     )
-    lax.fori_loop(
-        0,
-        jnp.maximum(rng[2 * tiles - 1] - 2 * tiles, 0),
-        projector(after, lin_after, weights, bias),
-        0,
-    )
+
+    def kept(side, tile):
+        _, scratch, out, _, _, base = side
+        some = pl.ds(slot_start(tile), SLOT_TILE)
+        return pltpu.make_async_copy(
+            scratch.at[:, some, :], out.at[:, some, :], sems.at[base + tile]
+        )
+
+    for side in reach:
+        project = projector(side[0], side[1], weights, bias)
+
+        def fill(tile, carry, side=side, project=project):
+            project(tile, carry)
+            kept(side, tile).start()
+            return carry
+
+        lax.fori_loop(side[3], side[4], fill, 0)
 
     def per_tile(tile, carry):
         first = slot_start(tile)
@@ -255,15 +267,15 @@
 
         @pl.when((low < end_before) | (start_after < end_after))
         def _():
-            make_queries(qa, lin, first, query_codes(fq, slot_start(tile + tiles)))
+            make_queries(qa, lin, first, query_codes(fq, first))
 
             def step_before(other, inner):
-                code = both(fk, slot_start(other), slice(0, LANES))
+                code = both(fk_before, slot_start(other), slice(0, LANES))
                 attend_step(qa, peak, acc, lin_before, slot_start(other), code)
                 return inner
 
             def step_after(other, inner):
-                code = both(fk, slot_start(other + 2 * tiles), slice(0, LANES))
+                code = both(fk_after, slot_start(other), slice(0, LANES))
                 attend_step(qa, peak, acc, lin_after, slot_start(other), code)
                 return inner
 
@@ -302,6 +314,13 @@
         return carry
 
     lax.fori_loop(0, tiles, per_tile, 0)
+    for side in reach:
+
+        def settle(tile, carry, side=side):
+            kept(side, tile).wait()
+            return carry
+
+        lax.fori_loop(side[3], side[4], settle, 0)
 
 
 def delta_kernel(d_ctx, ctx, stat, pay_out):
@@ -449,6 +468,12 @@
     ]
 
 
+def third(part, shape):
+    lead = (0,) * (len(shape) - 2)
+    block = shape[:-2] + (shape[-2] // 3, shape[-1])
+    return pl.BlockSpec(block, lambda _: lead + (part, 0))
+
+
 def attend_own(tok, weights, bias, fq, fk, rng):
     slots = tok.shape[1]
     tiles = slots // SLOT_TILE
@@ -462,7 +487,8 @@
         functools.partial(own_kernel, tiles),
         out_shape=tuple(jax.ShapeDtypeStruct(shape, kind) for shape, kind in shapes),
         grid=(1,),
-        in_specs=[SMEM] + [whole(item.shape) for item in (bias, fq, fk, weights, tok)],
+        in_specs=[SMEM, whole(bias.shape), third(1, fq.shape), third(1, fk.shape)]
+        + [whole(weights.shape), whole(tok.shape)],
         out_specs=tuple(whole(shape) for shape, _ in shapes),
         scratch_shapes=attend_scratch(),
         compiler_params=vmem(20),
@@ -485,14 +511,20 @@
         functools.partial(far_kernel, tiles),
         out_shape=tuple(jax.ShapeDtypeStruct(shape, kind) for shape, kind in shapes),
         grid=(1,),
-        in_specs=[SMEM]
-        + [whole(item.shape) for item in (bias, fq, fk, weights, before, after, *own)],
-        out_specs=tuple(whole(shape) for shape, _ in shapes),
-        scratch_shapes=attend_scratch(),
+        in_specs=[SMEM, whole(bias.shape), third(1, fq.shape), third(0, fk.shape)]
+        + [third(2, fk.shape), whole(weights.shape), whole(before.shape), whole(after.shape)]
+        + [whole((2, slots, WIDE)), whole(own[1].shape), whole(own[2].shape)],
+        out_specs=tuple(whole(shape) for shape, _ in shapes[:3]) + (ANY, ANY),
+        scratch_shapes=attend_scratch()
+        + [
+            pltpu.VMEM((2, slots, 3 * WIDE), BF),
+            pltpu.VMEM((2, slots, 3 * WIDE), BF),
+            pltpu.SemaphoreType.DMA((2 * tiles,)),
+        ],
         compiler_params=vmem(32),
         cost_estimate=cost(4, 8),
         name="attend_far",
-    )(rng, bias, fq, fk, weights, before, after, *own)
+    )(rng, bias, fq, fk, fk, weights, before, after, *own)
 
 
 def attend_back(lins, pays, fq, fk, rng):
@@ -564,15 +596,19 @@
 
 
 def chain_kernel(
-    tok, ctx_a, ctx_b, cot, wo_a, wo_b, vecs, up, up_bias, down,
+    tok, ctx_a, ctx_b, cot, wo_a, wo_b, vecs, up_from, up_bias, down_from,
     out, d_first_out, d_ctx_a, d_ctx_b, act_out, d_pre_out, normed_out, d_down_out, d_attn_out,
-    sums, up_sums, slope,
+    sums, up_sums, slope, up, down, sems,
 ):
     hidden = up.shape[1]
-    chunk = min(512, hidden)
+    chunk = min(256, hidden)
+    up_copy = pltpu.make_async_copy(up_from, up, sems.at[0])
+    down_copy = pltpu.make_async_copy(down_from, down, sems.at[1])
 
     @pl.when(pl.program_id(0) == 0)
     def _():
+        up_copy.start()
+        down_copy.start()
         sums[...] = jnp.zeros_like(sums)
         up_sums[...] = jnp.zeros_like(up_sums)
 
@@ -590,6 +626,12 @@
     normed = normal_1 * gain_1 + shift_1
     normed_r = normed.astype(BF)
     normed_out[...] = normed_r
+
+    @pl.when(pl.program_id(0) == 0)
+    def _():
+        up_copy.wait()
+        down_copy.wait()
+
     second = [normed + down_bias]
 
     def columns(part):
@@ -665,13 +707,18 @@
             whole(wo_a.shape),
             whole(wo_b.shape),
             whole(vecs.shape),
-            whole(up.shape),
+            pl.BlockSpec(memory_space=pltpu.HBM),
             whole(up_bias.shape),
-            whole(down.shape),
+            pl.BlockSpec(memory_space=pltpu.HBM),
         ],
         out_specs=tuple(row_block(rows, cols) for cols, _ in sizes)
         + (whole((8, model)), whole((8, hidden))),
-        scratch_shapes=[pltpu.VMEM((rows, hidden), F32)],
+        scratch_shapes=[
+            pltpu.VMEM((rows, hidden), F32),
+            pltpu.VMEM(up.shape, BF),
+            pltpu.VMEM(down.shape, BF),
+            pltpu.SemaphoreType.DMA((2,)),
+        ],
         compiler_params=vmem(28),
         cost_estimate=cost(6, 12),
         name="chain",

time: 340 us -> 337 us (level)
  Pallas kernels: 130 us -> 121 us
    pallas_call x2, Pallas kernels: 25.9 us -> 22.3 us  [attend_own(): pl.pallas_call(functools.partial(own_kernel, tiles), out_shape=tuple((jax...]
  transfers between devices with their start and end apart: 29 -> 29, of which waited for: 15 -> 14; matrix products, arithmetic and copies ran while one was open for 11% -> 11% of each run, Pallas kernels for 30% -> 28%
where the time goes in v2:
time: 337 us; the launch traced here: 331 us
  Pallas kernels  121 us (36%)
  starting transfers between devices  76.6 us (23%)
  waiting for transfers between devices  60.1 us (18%)
  local copies, waits for them, and re-layouts  28.2 us (8%)
  other arithmetic  22.5 us (7%)
  between operations  15.5 us (5%)
  matrix products  6.94 us (2%)
    ppermute x8, starting transfers between devices, shifted(): lax.ppermute(value, 'seq', [(i, i + by) for i in range(size) if 0 <= i +...  44 us
    pallas_call x2, Pallas kernels, attend_back(): pl.pallas_call(functools.partial(backward_kernel, tiles), out_shape=jax.S...  37.4 us
    ppermute x12, waiting for transfers between devices, moved(): return lax.ppermute(value, ('seg', 'seq'), pairs)  30 us
    psum x1, waiting for transfers between devices, per_device(): grads = lax.psum(grads, ('seg', 'seq'))  24.7 us
    pallas_call x2, Pallas kernels, attend_own(): pl.pallas_call(functools.partial(own_kernel, tiles), out_shape=tuple((jax...  22.3 us
    ppermute x12, starting transfers between devices, moved(): return lax.ppermute(value, ('seg', 'seq'), pairs)  21.8 us
    pallas_call x2, Pallas kernels, chain(): pl.pallas_call(chain_kernel, out_shape=tuple((jax.ShapeDtypeStruct((slots...  21.1 us
    pallas_call x2, Pallas kernels, attend_far(): pl.pallas_call(functools.partial(far_kernel, tiles), out_shape=tuple((jax...  14.9 us
  transfers between devices with their start and end apart: 29, of which 14 were waited for; matrix products, arithmetic and copies ran while one was open for 11% of the time, Pallas kernels for 28%

profile of v2, /device:TPU:0, one launch (start us, length us, event | category | flops | bytes accessed | tf_op | source)
XLA Modules:
  0.0 331.2 jit_solution(3908475430581202077)
XLA Ops:
  7.3 2.4 slice_bitcast_fusion.7
  9.7 2.9 collective-permute-start.16
  14.7 2.3 or_and_fusion
  17.0 4.0 %select_convert_fusion = bf16[2,1536,128]{2,1,0:T(8,128)(2,1)} fusion(pred[128]{0:T(512)(128)(4,1)S(1)} %get-tuple-element.438, pred[2,1536]{1,0:T(4,128)(4,1)S(1)} %get-tuple-element.429, s32[2,1536]{1,0:T(2,128)S(1)} %get-tuple-element.426, s32[2,1536]{1,0:T(2,128)S(1)} %get-tuple-element.427, s32[2,1536]{1,0:T(2,128)S(1)} %get-tuple-element.425, ...), kind=kLoop, calls=%fused_computation.52 | loop fusion | flops 3932160 | bytes 827008 | tf_op jit(solution)/shard_map/convert_element_type | solution.py:1027
  21.0 1.6 copy.92
  22.6 1.1 or_convert_fusion
  24.9 2.5 maximum_select_fusion.1.tok
  27.4 1.3 collective-permute-start.19
  28.7 4.0 %collective-permute-start.18 = (bf16[2,512,512]{2,1,0:T(8,128)(2,1)}, bf16[2,512,512]{2,1,0:T(8,128)(2,1)}, u32[]{:S(2)}, u32[]{:S(2)}) collective-permute-start(bf16[2,512,512]{2,1,0:T(8,128)(2,1)} %maximum_select_fusion.1.tok), channel_id=1, source_target_pairs={{0,1},{1,2},{2,3},{3,4},{4,5},{5,6},{6,7},{7,8},{8,9},{9,10},{10,1... | collective-permute-start | bytes 3145736 | tf_op jit(solution)/shard_map/ppermute | solution.py:913
  33.6 1.6 collective-permute-start.17
  35.2 1.2 slice_bitcast_fusion.10
  36.4 10.6 %attend_own.2 = (bf16[2,512,768]{2,1,0:T(8,128)(2,1)}, f32[4,4,256,128]{3,2,1,0:T(8,128)S(1)}, f32[4,256,128]{2,1,0:T(8,128)S(1)}) custom-call(s32[8]{0:T(128)S(1)} %squeeze.81.rng, f32[8,768]{1,0:T(8,128)S(1)} %broadcast_in_dim.170.bias, bf16[1536,128]{1,0:T(8,128)(2,1)S(1)} %get-tuple-element.409.fq, ...), custom_call_target="tpu_custom_call" | custom-call | flops 1000000000 | bytes 1000000 | tf_op jit(solution)/shard_map/attend_own/pallas_call | solution.py:486
  48.0 1.4 maximum_select_fusion.tok
  49.5 11.7 %attend_own.3 = (bf16[2,512,768]{2,1,0:T(8,128)(2,1)}, f32[4,4,256,128]{3,2,1,0:T(8,128)S(1)}, f32[4,256,128]{2,1,0:T(8,128)S(1)}) custom-call(s32[8]{0:T(128)S(1)} %squeeze.86.rng, f32[8,768]{1,0:T(8,128)S(1)} %broadcast_in_dim.170.bias, bf16[1536,128]{1,0:T(8,128)(2,1)S(1)} %get-tuple-element.410.fq, ...), custom_call_target="tpu_custom_call" | custom-call | flops 1000000000 | bytes 1000000 | tf_op jit(solution)/shard_map/attend_own/pallas_call | solution.py:486
  61.2 1.3 copy-done.9
  63.3 1.3 collective-permute-start.22
  64.6 4.0 %collective-permute-start.21 = (bf16[2,512,512]{2,1,0:T(8,128)(2,1)}, bf16[2,512,512]{2,1,0:T(8,128)(2,1)}, u32[]{:S(2)}, u32[]{:S(2)}) collective-permute-start(bf16[2,512,512]{2,1,0:T(8,128)(2,1)} %maximum_select_fusion.tok), channel_id=1, source_target_pairs={{0,1},{1,2},{2,3},{3,4},{4,5},{5,6},{6,7},{7,8},{8,9},{9,10},{10,1... | collective-permute-start | bytes 3145736 | tf_op jit(solution)/shard_map/ppermute | solution.py:913
  68.8 1.1 dynamic-slice_bitcast_fusion.4
  69.9 1.6 copy-done.12
  72.5 5.9 %attend_far.2 = (f32[2,512,256]{2,1,0:T(8,128)S(1)}, bf16[2,512,256]{2,1,0:T(8,128)(2,1)S(1)}, bf16[2,512,128]{2,1,0:T(8,128)(2,1)S(1)}, bf16[2,512,768]{2,1,0:T(8,128)(2,1)}, bf16[2,512,768]{2,1,0:T(8,128)(2,1)}) custom-call(s32[8]{0:T(128)S(1)} %squeeze.81.rng, f32[8,768]{1,0:T(8,128)S(1)} %broadcast_in_dim.170.bias, ...), custom_call_target="tpu_custom_call" | custom-call | flops 4000000000 | bytes 8000000 | tf_op jit(solution)/shard_map/attend_far/pallas_call | solution.py:510
  78.6 1.2 collective-permute-start.20
  79.9 8.9 %attend_far.3 = (f32[2,512,256]{2,1,0:T(8,128)S(1)}, bf16[2,512,256]{2,1,0:T(8,128)(2,1)S(1)}, bf16[2,512,128]{2,1,0:T(8,128)(2,1)S(1)}, bf16[2,512,768]{2,1,0:T(8,128)(2,1)}, bf16[2,512,768]{2,1,0:T(8,128)(2,1)}) custom-call(s32[8]{0:T(128)S(1)} %squeeze.86.rng, f32[8,768]{1,0:T(8,128)S(1)} %broadcast_in_dim.170.bias, ...), custom_call_target="tpu_custom_call" | custom-call | flops 4000000000 | bytes 8000000 | tf_op jit(solution)/shard_map/attend_far/pallas_call | solution.py:510
  88.8 10.6 %chain.2 = (bf16[512,512]{1,0:T(8,128)(2,1)S(1)}, f32[512,512]{1,0:T(8,128)}, bf16[512,256]{1,0:T(8,128)(2,1)S(1)}, bf16[512,256]{1,0:T(8,128)(2,1)S(1)}, bf16[5...) custom-call(bf16[2,1,512,512]{3,2,1,0:T(8,128)(2,1)S(1)} %copy-done., ...), custom_call_target="tpu_custom_call" | custom-call | flops 6000000000 | bytes 12000000 | tf_op jit(solution)/shard_map/chain/pallas_call | solution.py:697
  100.3 1.3 collective-permute-start.23
  101.6 4.2 %collective-permute-done.24 = bf16[512,256]{1,0:T(8,128)(2,1)S(1)} collective-permute-done((bf16[512,256]{1,0:T(8,128)(2,1)S(1)}, bf16[512,256]{1,0:T(8,128)(2,1)S(1)}, u32[]{:S(2)}, u32[]{:S(2)}) %collective-permute-start.24) | collective-permute-done | bytes 262176 | tf_op jit(solution)/shard_map/ppermute | solution.py:908
  105.9 1.8 payload.2
  108.7 10.5 %chain.3 = (bf16[512,512]{1,0:T(8,128)(2,1)S(1)}, f32[512,512]{1,0:T(8,128)}, bf16[512,256]{1,0:T(8,128)(2,1)S(1)}, bf16[512,256]{1,0:T(8,128)(2,1)S(1)}, bf16[5...) custom-call(bf16[2,1,512,512]{3,2,1,0:T(8,128)(2,1)S(1)} %copy-done., ...), custom_call_target="tpu_custom_call" | custom-call | flops 6000000000 | bytes 12000000 | tf_op jit(solution)/shard_map/chain/pallas_call | solution.py:697
  119.2 1.3 collective-permute-start.27
  120.5 26.6 %collective-permute-start.26 = (bf16[2,512,384]{2,1,0:T(8,128)(2,1)}, bf16[2,512,384]{2,1,0:T(8,128)(2,1)}, u32[]{:S(2)}, u32[]{:S(2)}) collective-permute-start(bf16[2,512,384]{2,1,0:T(8,128)(2,1)} %payload.2), channel_id=1, source_target_pairs={{0,1},{1,2},{2,3},{3,4},{4,5},{5,6},{6,7},{7,8},{8,9},{9,10},{10,1... | collective-permute-start | bytes 2359304 | tf_op jit(solution)/shard_map/ppermute | solution.py:913
  147.8 8.7 %weight_grads.1 = bf16[4624,512]{1,0:T(8,128)(2,1)} custom-call(bf16[512,2048]{1,0:T(8,128)(2,1)S(1)} %get-tuple-element.197.refs_0_, bf16[512,2048]{1,0:T(8,128)(2,1)S(1)} %get-tuple-element.198.refs_1_, bf16[512,512]{1,0:T(8,128)(2,1)S(1)} %get-tuple-element.199.refs_2_, bf16[512,512]{1,0:T(8,128)(2,1)S(1)} %get-tuple-element.200.refs_3_, ...), custom_call_target="tpu_custom_call" | custom-call | flops 1000000000 | bytes 2000000 | tf_op jit(solution)/shard_map/weight_grads/pallas_call | solution.py:783
  157.7 1.1 maximum_bitcast_fusion.1
  158.9 1.9 payload.3
  160.8 128.5 %conditional.1 = (f32[2,1,512,512]{3,2,1,0:T(8,128)}, f32[512,1536]{1,0:T(8,128)}, f32[16,1024]{1,0:T(8,128)}, f32[1,512]{1,0:T(1,128)}, f32[1,512]{1,0:T(1,128)}, /*index=5*/f32[512]{0:T(512)S(1)}, f32[512]{0:T(512)S(1)}) conditional(s32[]{:T(128)} %bitcast.72, () %tuple.27, (s32[]{:T(128)}, s32[]{:T(128)}, s32[2,4,2]{1,0,2:T(2,128)S(1)}, ...), branch_computations={%region_6.7_spmd, %region_7.8_spmd} | conditional | flops 51318296576 | bytes 140407264 | solution.py:1164
  160.8 1.3 collective-permute-start.1
  162.1 4.2 %collective-permute-start = (bf16[2,512,384]{2,1,0:T(8,128)(2,1)}, bf16[2,512,384]{2,1,0:T(8,128)(2,1)}, u32[]{:S(2)}, u32[]{:S(2)}) collective-permute-start(bf16[2,512,384]{2,1,0:T(8,128)(2,1)} %get-tuple-element.58.rest_1_), channel_id=1, source_target_pairs={{0,1},{1,2},{2,3},{3,4},{4,5},{5,6},{6,7},{7,8},{8,9},{9,10},{10,1... | collective-permute-start | bytes 2359304 | tf_op jit(solution)/shard_map/cond/branch_1_fun/ppermute | solution.py:913
  166.5 1.3 slice_bitcast_fusion.2
  168.1 1.2 copy-done.38
  169.8 14.8 %attend_back.2.refs_2_ = bf16[2,512,768]{2,1,0:T(8,128)(2,1)S(1)} custom-call(s32[8]{0:T(128)S(1)} %squeeze.29.rng, bf16[1536,128]{1,0:T(8,128)(2,1)S(1)} %get-tuple-element.388.fq, bf16[2,1536,128]{2,1,0:T(8,128)(2,1)S(1)} %get-tuple-element.384.fk, bf16[2,512,384]{2,1,0:T(8,128)(2,1)} %get-tuple-element.52.rest_0_, ...), custom_call_target="tpu_custom_call" | custom-call | flops 24000000000 | bytes 12000000 | tf_op jit(solution)/shard_map/cond/branch_1_fun/attend_back/pallas_call | solution.py:534
  184.6 2.5 convolution_convert_fusion.1
  187.1 1.4 collective-permute-start.2
  188.5 22.6 %attend_back.3.refs_3_ = bf16[2,512,768]{2,1,0:T(8,128)(2,1)S(1)} custom-call(s32[8]{0:T(128)S(1)} %squeeze.62.rng, bf16[1536,128]{1,0:T(8,128)(2,1)S(1)} %get-tuple-element.387.fq, bf16[2,1536,128]{2,1,0:T(8,128)(2,1)S(1)} %get-tuple-element.383.fk, bf16[2,512,384]{2,1,0:T(8,128)(2,1)} %collective-permute-done.rest_0_, ...), custom_call_target="tpu_custom_call" | custom-call | flops 24000000000 | bytes 12000000 | tf_op jit(solution)/shard_map/cond/branch_1_fun/attend_back/pallas_call | solution.py:534
  211.2 4.5 %qkv_weight_grad.1 = bf16[640,768]{1,0:T(8,128)(2,1)S(1)} custom-call(bf16[2,512,512]{2,1,0:T(8,128)(2,1)} %get-tuple-element.47.refs_0_, bf16[2,512,512]{2,1,0:T(8,128)(2,1)} %get-tuple-element.48.refs_1_, bf16[2,512,768]{2,1,0:T(8,128)(2,1)S(1)} %attend_back.2.refs_2_, bf16[2,512,768]{2,1,0:T(8,128)(2,1)S(1)} %attend_back.3.refs_3_, ...), custom_call_target="tpu_custom_call" | custom-call | flops 1600000000 | bytes 4000000 | tf_op jit(solution)/shard_map/cond/branch_1_fun/qkv_weight_grad/pallas_call | solution.py:854
  216.5 9.8 %collective-permute-start.3 = (bf16[8,40,768]{2,1,0:T(8,128)(2,1)}, bf16[8,40,768]{2,1,0:T(8,128)(2,1)}, u32[]{:S(2)}, u32[]{:S(2)}) collective-permute-start(bf16[8,40,768]{2,1,0:T(8,128)(2,1)} %dynamic-slice_bitcast_fusion), channel_id=1, source_target_pairs={{0,1},{1,0},{2,3},{3,2},{4,5},{5,4},{6,7},{7,6},{8,9},{9,8},{10,11... | collective-permute-start | bytes 1474568 | tf_op jit(solution)/shard_map/cond/branch_1_fun/ppermute | solution.py:951
  226.3 1.8 collective-permute-done.3
  228.1 1.1 fusion
  229.4 1.8 convolution_convert_fusion
  232.0 5.6 %collective-permute-done.4 = bf16[4,40,768]{2,1,0:T(8,128)(2,1)S(1)} collective-permute-done((bf16[4,40,768]{2,1,0:T(8,128)(2,1)S(1)}, bf16[4,40,768]{2,1,0:T(8,128)(2,1)S(1)}, u32[]{:S(2)}, u32[]{:S(2)}) %collective-permute-start.4) | collective-permute-done | bytes 245792 | tf_op jit(solution)/shard_map/cond/branch_1_fun/ppermute | solution.py:951
  237.7 2.5 collective-permute-start.5
  240.5 1.3 collective-permute-start.6
  243.1 3.4 %collective-permute-done.7 = bf16[1,40,768]{2,1,0:T(8,128)(2,1)S(1)} collective-permute-done((bf16[1,40,768]{2,1,0:T(8,128)(2,1)S(1)}, bf16[1,40,768]{2,1,0:T(8,128)(2,1)S(1)}, u32[]{:S(2)}, u32[]{:S(2)}) %collective-permute-start.7) | collective-permute-done | bytes 61472 | tf_op jit(solution)/shard_map/cond/branch_1_fun/ppermute | solution.py:951
  246.5 2.6 collective-permute-done.6
  252.0 2.4 collective-permute-start.9
  254.6 3.7 %collective-permute-done.10 = bf16[1,40,768]{2,1,0:T(8,128)(2,1)S(1)} collective-permute-done((bf16[1,40,768]{2,1,0:T(8,128)(2,1)S(1)}, bf16[1,40,768]{2,1,0:T(8,128)(2,1)S(1)}, u32[]{:S(2)}, u32[]{:S(2)}) %collective-permute-start.10) | collective-permute-done | bytes 61472 | tf_op jit(solution)/shard_map/cond/branch_1_fun/ppermute | solution.py:951
  262.0 2.0 collective-permute-start.12
  264.0 8.8 %collective-permute-done.14 = bf16[4,40,768]{2,1,0:T(8,128)(2,1)} collective-permute-done((bf16[4,40,768]{2,1,0:T(8,128)(2,1)}, bf16[4,40,768]{2,1,0:T(8,128)(2,1)}, u32[]{:S(2)}, u32[]{:S(2)}) %collective-permute-start.14) | collective-permute-done | bytes 245792 | tf_op jit(solution)/shard_map/cond/branch_1_fun/ppermute | solution.py:951
  273.8 2.2 collective-permute-done.12
  276.0 1.1 select_bitcast_fusion.5
  278.2 2.0 convolution_add_fusion.refs_0_
  281.2 1.6 select_bitcast_fusion.1
  283.8 2.7 finish.1
  286.6 1.3 fusion.23
  289.3 24.7 %all-reduce.2.cloned.1.call-done.cells = bf16[4624,512]{1,0:T(8,128)(2,1)} async-done(((bf16[4624,512]{1,0:T(8,128)(2,1)}), bf16[4624,512]{1,0:T(8,128)(2,1)}) %all-reduce.2.cloned.1.call-update) | async-done | bytes 4734992 | tf_op jit(solution)/shard_map/psum | solution.py:1152
  315.9 2.3 copy-done
  318.3 5.9 %unpack.1 = (f32[2048,512]{1,0:T(8,128)}, f32[512,2048]{1,0:T(8,128)}, f32[512,512]{1,0:T(8,128)}) custom-call(bf16[4624,512]{1,0:T(8,128)(2,1)S(1)} %copy-done), custom_call_target="tpu_custom_call" | custom-call | flops 100000000 | bytes 16000000 | tf_op jit(solution)/shard_map/unpack/pallas_call | solution.py:815
  (181 shorter events, 29.0 us)
Async XLA Ops:
  7.2 5.5 %copy-start.36 = (bf16[512]{0:T(512)(128)(2,1)S(1)}, bf16[512]{0:T(512)(128)(2,1)}, u32[]{:S(2)}) copy-start(bf16[512]{0:T(512)(128)(2,1)} %param.21) | copy-start | bytes 3076
  7.2 5.5 %copy-start.37 = (bf16[512]{0:T(512)(128)(2,1)S(1)}, bf16[512]{0:T(512)(128)(2,1)}, u32[]{:S(2)}) copy-start(bf16[512]{0:T(512)(128)(2,1)} %param.22) | copy-start | bytes 3076
  7.2 5.5 %copy-start.29 = (s32[2,2,96]{2,1,0:T(2,128)S(1)}, s32[2,2,96]{2,1,0:T(2,128)}, u32[]{:S(2)}) copy-start(s32[2,2,96]{2,1,0:T(2,128)} %param.19) | copy-start | bytes 4612
  7.2 13.8 %copy-start.23 = (bf16[512,1536]{1,0:T(8,128)(2,1)S(1)}, bf16[512,1536]{1,0:T(8,128)(2,1)}, u32[]{:S(2)}) copy-start(bf16[512,1536]{1,0:T(8,128)(2,1)} %param.20) | copy-start | bytes 4718596
  7.2 306.8 %all-reduce.2.cloned.1.call-start = ((), (), s32[]{:S(2)}) async-start(), calls=%async_computation | async-start | bytes 9469952 | tf_op jit(solution)/shard_map/psum | solution.py:1152
  9.7 15.2 %collective-permute-start.16 = (bf16[512,512]{1,0:T(8,128)(2,1)}, bf16[512,512]{1,0:T(8,128)(2,1)}, u32[]{:S(2)}, u32[]{:S(2)}) collective-permute-start(bf16[512,512]{1,0:T(8,128)(2,1)} %get-tuple-element.407), channel_id=1, source_target_pairs={{0,16},{16,0},{1,17},{17,1},{2,18},{18,2},{3,19},{19,3},{4,20},{20... | collective-permute-start | bytes 1572872 | tf_op jit(solution)/shard_map/ppermute | solution.py:908
  23.7 1.2 copy-start.17
  24.9 7.8 %copy-start.21 = (bf16[512,1536]{0,1:T(8,128)(2,1)S(1)}, bf16[512,1536]{0,1:T(8,128)(2,1)}, u32[]{:S(2)}) copy-start(bf16[512,1536]{0,1:T(8,128)(2,1)} %copy.92) | copy-start | bytes 4718596
  27.4 35.9 %collective-permute-start.19 = (bf16[2,512,512]{2,1,0:T(8,128)(2,1)}, bf16[2,512,512]{2,1,0:T(8,128)(2,1)}, u32[]{:S(2)}, u32[]{:S(2)}) collective-permute-start(bf16[2,512,512]{2,1,0:T(8,128)(2,1)} %maximum_select_fusion.1.tok), channel_id=1, source_target_pairs={{1,0},{2,1},{3,2},{4,3},{5,4},{6,5},{7,6},{8,7},{9,8},{10,9},{11,1... | collective-permute-start | bytes 3145736 | tf_op jit(solution)/shard_map/ppermute | solution.py:913
  28.7 34.7 %collective-permute-start.18 = (bf16[2,512,512]{2,1,0:T(8,128)(2,1)}, bf16[2,512,512]{2,1,0:T(8,128)(2,1)}, u32[]{:S(2)}, u32[]{:S(2)}) collective-permute-start(bf16[2,512,512]{2,1,0:T(8,128)(2,1)} %maximum_select_fusion.1.tok), channel_id=1, source_target_pairs={{0,1},{1,2},{2,3},{3,4},{4,5},{5,6},{6,7},{7,8},{8,9},{9,10},{10,1... | collective-permute-start | bytes 3145736 | tf_op jit(solution)/shard_map/ppermute | solution.py:913
  33.6 14.4 %collective-permute-start.17 = (bf16[512,512]{1,0:T(8,128)(2,1)}, bf16[512,512]{1,0:T(8,128)(2,1)S(1)}, u32[]{:S(2)}, u32[]{:S(2)}) collective-permute-start(bf16[512,512]{1,0:T(8,128)(2,1)} %get-tuple-element.160), channel_id=1, source_target_pairs={{0,16},{16,0},{1,17},{17,1},{2,18},{18,2},{3,19},{19,3},{4,20},{20... | collective-permute-start | bytes 1572872 | tf_op jit(solution)/shard_map/ppermute | solution.py:908
  36.4 11.6 %copy-start.22 = (bf16[512,512]{1,0:T(8,128)(2,1)S(1)}, bf16[512,512]{1,0:T(8,128)(2,1)}, u32[]{:S(2)}) copy-start(bf16[512,512]{1,0:T(8,128)(2,1)} %get-tuple-element.160) | copy-start | bytes 1572868
  47.8 1.7 copy-start.11
  49.4 19.2 %copy-start.30 = (bf16[512]{0:T(512)(128)(2,1)S(1)}, bf16[512]{0:T(512)(128)(2,1)}, u32[]{:S(2)}) copy-start(bf16[512]{0:T(512)(128)(2,1)} %param.24) | copy-start | bytes 3076
  49.4 19.2 %copy-start.31 = (bf16[512]{0:T(512)(128)(2,1)S(1)}, bf16[512]{0:T(512)(128)(2,1)}, u32[]{:S(2)}) copy-start(bf16[512]{0:T(512)(128)(2,1)} %param.25) | copy-start | bytes 3076
  49.4 19.2 %copy-start.32 = (bf16[512]{0:T(512)(128)(2,1)S(1)}, bf16[512]{0:T(512)(128)(2,1)}, u32[]{:S(2)}) copy-start(bf16[512]{0:T(512)(128)(2,1)} %param.26) | copy-start | bytes 3076
  49.4 19.2 %copy-start.33 = (bf16[512]{0:T(512)(128)(2,1)S(1)}, bf16[512]{0:T(512)(128)(2,1)}, u32[]{:S(2)}) copy-start(bf16[512]{0:T(512)(128)(2,1)} %param.30) | copy-start | bytes 3076
  49.4 19.2 %copy-start.34 = (bf16[512]{0:T(512)(128)(2,1)S(1)}, bf16[512]{0:T(512)(128)(2,1)}, u32[]{:S(2)}) copy-start(bf16[512]{0:T(512)(128)(2,1)} %param.31) | copy-start | bytes 3076
  49.5 19.3 %copy-start.35 = (bf16[512]{0:T(512)(128)(2,1)S(1)}, bf16[512]{0:T(512)(128)(2,1)}, u32[]{:S(2)}) copy-start(bf16[512]{0:T(512)(128)(2,1)} %param.32) | copy-start | bytes 3076
  49.5 19.3 %copy-start.26 = (bf16[2048]{0:T(1024)(128)(2,1)S(1)}, bf16[2048]{0:T(1024)(128)(2,1)}, u32[]{:S(2)}) copy-start(bf16[2048]{0:T(1024)(128)(2,1)} %param.28) | copy-start | bytes 12292
  61.2 1.3 copy-start.9
  63.3 16.5 %collective-permute-start.22 = (bf16[2,512,512]{2,1,0:T(8,128)(2,1)}, bf16[2,512,512]{2,1,0:T(8,128)(2,1)}, u32[]{:S(2)}, u32[]{:S(2)}) collective-permute-start(bf16[2,512,512]{2,1,0:T(8,128)(2,1)} %maximum_select_fusion.tok), channel_id=1, source_target_pairs={{1,0},{2,1},{3,2},{4,3},{5,4},{6,5},{7,6},{8,7},{9,8},{10,9},{11,1... | collective-permute-start | bytes 3145736 | tf_op jit(solution)/shard_map/ppermute | solution.py:913
  64.6 15.2 %collective-permute-start.21 = (bf16[2,512,512]{2,1,0:T(8,128)(2,1)}, bf16[2,512,512]{2,1,0:T(8,128)(2,1)}, u32[]{:S(2)}, u32[]{:S(2)}) collective-permute-start(bf16[2,512,512]{2,1,0:T(8,128)(2,1)} %maximum_select_fusion.tok), channel_id=1, source_target_pairs={{0,1},{1,2},{2,3},{3,4},{4,5},{5,6},{6,7},{7,8},{8,9},{9,10},{10,1... | collective-permute-start | bytes 3145736 | tf_op jit(solution)/shard_map/ppermute | solution.py:913
  69.9 1.6 copy-start.12
  72.5 7.3 %copy-start.10 = (f32[4,4,256,128]{3,2,1,0:T(8,128)S(1)}, f32[4,4,256,128]{3,2,1,0:T(8,128)}, u32[]{:S(2)}) copy-start(f32[4,4,256,128]{3,2,1,0:T(8,128)} %copy-done.9) | copy-start | bytes 6291460
  72.5 7.3 %copy-start.14 = (f32[4,256,128]{2,1,0:T(8,128)S(1)}, f32[4,256,128]{2,1,0:T(8,128)}, u32[]{:S(2)}) copy-start(f32[4,256,128]{2,1,0:T(8,128)} %copy-done.13) | copy-start | bytes 1572868
  72.5 7.3 %copy-start.39 = (bf16[2,512,768]{2,1,0:T(8,128)(2,1)S(1)}, bf16[2,512,768]{2,1,0:T(8,128)(2,1)}, u32[]{:S(2)}) copy-start(bf16[2,512,768]{2,1,0:T(8,128)(2,1)} %get-tuple-element.179.lin) | copy-start | bytes 4718596
  78.5 10.3 %copy-start.3 = (bf16[2,1,512,512]{3,2,1,0:T(8,128)(2,1)S(1)}, bf16[2,1,512,512]{3,2,1,0:T(8,128)(2,1)}, u32[]{:S(2)}) copy-start(bf16[2,1,512,512]{3,2,1,0:T(8,128)(2,1)} %tok.3) | copy-start | bytes 3145732
  78.5 10.3 %copy-start.6 = (bf16[512,2048]{1,0:T(8,128)(2,1)S(1)}, bf16[512,2048]{1,0:T(8,128)(2,1)}, u32[]{:S(2)}) copy-start(bf16[512,2048]{1,0:T(8,128)(2,1)} %up_from.3) | copy-start | bytes 6291460
  78.6 10.3 %copy-start.7 = (bf16[2048,512]{1,0:T(8,128)(2,1)S(1)}, bf16[2048,512]{1,0:T(8,128)(2,1)}, u32[]{:S(2)}) copy-start(bf16[2048,512]{1,0:T(8,128)(2,1)} %down_from.3) | copy-start | bytes 6291460
  78.6 10.3 %copy-start.8 = (bf16[2,1,512,512]{3,2,1,0:T(8,128)(2,1)S(1)}, bf16[2,1,512,512]{3,2,1,0:T(8,128)(2,1)}, u32[]{:S(2)}) copy-start(bf16[2,1,512,512]{3,2,1,0:T(8,128)(2,1)} %cot.3) | copy-start | bytes 3145732
  78.6 10.2 %collective-permute-start.20 = (bf16[512,256]{1,0:T(8,128)(2,1)S(1)}, bf16[512,256]{1,0:T(8,128)(2,1)S(1)}, u32[]{:S(2)}, u32[]{:S(2)}) collective-permute-start(bf16[512,256]{1,0:T(8,128)(2,1)S(1)} %get-tuple-element.411), channel_id=1, source_target_pairs={{0,16},{16,0},{1,17},{17,1},{2,18},{18,2},{3,19},{19,3},{4,20},{20... | collective-permute-start | bytes 786440 | tf_op jit(solution)/shard_map/ppermute | solution.py:908
  99.4 6.4 %collective-permute-start.24 = (bf16[512,256]{1,0:T(8,128)(2,1)S(1)}, bf16[512,256]{1,0:T(8,128)(2,1)S(1)}, u32[]{:S(2)}, u32[]{:S(2)}) collective-permute-start(bf16[512,256]{1,0:T(8,128)(2,1)S(1)} %get-tuple-element.194), channel_id=1, source_target_pairs={{0,16},{16,0},{1,17},{17,1},{2,18},{18,2},{3,19},{19,3},{4,20},{20... | collective-permute-start | bytes 786440 | tf_op jit(solution)/shard_map/ppermute | solution.py:908
  100.3 8.3 %collective-permute-start.23 = (bf16[512,256]{1,0:T(8,128)(2,1)S(1)}, bf16[512,256]{1,0:T(8,128)(2,1)S(1)}, u32[]{:S(2)}, u32[]{:S(2)}) collective-permute-start(bf16[512,256]{1,0:T(8,128)(2,1)S(1)} %get-tuple-element.415), channel_id=1, source_target_pairs={{0,16},{16,0},{1,17},{17,1},{2,18},{18,2},{3,19},{19,3},{4,20},{20... | collective-permute-start | bytes 786440 | tf_op jit(solution)/shard_map/ppermute | solution.py:908
  119.2 37.4 %collective-permute-start.27 = (bf16[2,512,384]{2,1,0:T(8,128)(2,1)}, bf16[2,512,384]{2,1,0:T(8,128)(2,1)}, u32[]{:S(2)}, u32[]{:S(2)}) collective-permute-start(bf16[2,512,384]{2,1,0:T(8,128)(2,1)} %payload.2), channel_id=1, source_target_pairs={{1,0},{2,1},{3,2},{4,3},{5,4},{6,5},{7,6},{8,7},{9,8},{10,9},{11,1... | collective-permute-start | bytes 2359304 | tf_op jit(solution)/shard_map/ppermute | solution.py:913
  120.5 36.1 %collective-permute-start.26 = (bf16[2,512,384]{2,1,0:T(8,128)(2,1)}, bf16[2,512,384]{2,1,0:T(8,128)(2,1)}, u32[]{:S(2)}, u32[]{:S(2)}) collective-permute-start(bf16[2,512,384]{2,1,0:T(8,128)(2,1)} %payload.2), channel_id=1, source_target_pairs={{0,1},{1,2},{2,3},{3,4},{4,5},{5,6},{6,7},{7,8},{8,9},{9,10},{10,1... | collective-permute-start | bytes 2359304 | tf_op jit(solution)/shard_map/ppermute | solution.py:913
  147.1 9.5 %collective-permute-start.25 = (bf16[512,256]{1,0:T(8,128)(2,1)S(1)}, bf16[512,256]{1,0:T(8,128)(2,1)S(1)}, u32[]{:S(2)}, u32[]{:S(2)}) collective-permute-start(bf16[512,256]{1,0:T(8,128)(2,1)S(1)} %get-tuple-element.211), channel_id=1, source_target_pairs={{0,16},{16,0},{1,17},{17,1},{2,18},{18,2},{3,19},{19,3},{4,20},{20... | collective-permute-start | bytes 786440 | tf_op jit(solution)/shard_map/ppermute | solution.py:908
  158.9 1.9 copy-start.18
  160.8 27.8 %collective-permute-start.1 = (bf16[2,512,384]{2,1,0:T(8,128)(2,1)}, bf16[2,512,384]{2,1,0:T(8,128)(2,1)}, u32[]{:S(2)}, u32[]{:S(2)}) collective-permute-start(bf16[2,512,384]{2,1,0:T(8,128)(2,1)} %get-tuple-element.58.rest_1_), channel_id=1, source_target_pairs={{1,0},{2,1},{3,2},{4,3},{5,4},{6,5},{7,6},{8,7},{9,8},{10,9},{11,1... | collective-permute-start | bytes 2359304 | tf_op jit(solution)/shard_map/cond/branch_1_fun/ppermute | solution.py:913
  162.1 26.5 %collective-permute-start = (bf16[2,512,384]{2,1,0:T(8,128)(2,1)}, bf16[2,512,384]{2,1,0:T(8,128)(2,1)}, u32[]{:S(2)}, u32[]{:S(2)}) collective-permute-start(bf16[2,512,384]{2,1,0:T(8,128)(2,1)} %get-tuple-element.58.rest_1_), channel_id=1, source_target_pairs={{0,1},{1,2},{2,3},{3,4},{4,5},{5,6},{6,7},{7,8},{8,9},{9,10},{10,1... | collective-permute-start | bytes 2359304 | tf_op jit(solution)/shard_map/cond/branch_1_fun/ppermute | solution.py:913
  166.5 1.6 copy-start.41
  167.8 1.5 copy-start.38
  167.8 2.0 copy-start.40
  187.1 24.1 %collective-permute-start.2 = (bf16[512,512]{1,0:T(8,128)(2,1)}, bf16[512,512]{1,0:T(8,128)(2,1)S(1)}, u32[]{:S(2)}, u32[]{:S(2)}) collective-permute-start(bf16[512,512]{1,0:T(8,128)(2,1)} %convolution_convert_fusion.1), channel_id=1, source_target_pairs={{0,16},{16,0},{1,17},{17,1},{2,18},{18,2},{3,19},{19,3},{4,20},{20... | collective-permute-start | bytes 1572872 | tf_op jit(solution)/shard_map/cond/branch_1_fun/ppermute | solution.py:908
  211.2 4.5 %copy-start.1 = (bf16[2,512,768]{2,1,0:T(8,128)(2,1)}, bf16[2,512,768]{2,1,0:T(8,128)(2,1)S(1)}, u32[]{:S(2)}) copy-start(bf16[2,512,768]{2,1,0:T(8,128)(2,1)S(1)} %attend_back.3.refs_3_) | copy-start | bytes 4718596 | tf_op jit(solution)/shard_map/cond
  216.5 11.6 %collective-permute-start.3 = (bf16[8,40,768]{2,1,0:T(8,128)(2,1)}, bf16[8,40,768]{2,1,0:T(8,128)(2,1)}, u32[]{:S(2)}, u32[]{:S(2)}) collective-permute-start(bf16[8,40,768]{2,1,0:T(8,128)(2,1)} %dynamic-slice_bitcast_fusion), channel_id=1, source_target_pairs={{0,1},{1,0},{2,3},{3,2},{4,5},{5,4},{6,7},{7,6},{8,9},{9,8},{10,11... | collective-permute-start | bytes 1474568 | tf_op jit(solution)/shard_map/cond/branch_1_fun/ppermute | solution.py:951
  226.3 3.1 copy-start.2
  229.3 12.5 %copy-start.20 = (bf16[512,768]{0,1:T(8,128)(2,1)S(1)}, bf16[512,768]{0,1:T(8,128)(2,1)}, u32[]{:S(2)}) copy-start(bf16[512,768]{0,1:T(8,128)(2,1)} %get-tuple-element.354) | copy-start | bytes 2359300 | tf_op jit(solution)/shard_map/cond
  229.3 12.5 %copy-start.24 = (f32[512,512]{1,0:T(8,128)S(1)}, f32[512,512]{1,0:T(8,128)}, u32[]{:S(2)}) copy-start(f32[512,512]{1,0:T(8,128)} %get-tuple-element.63) | copy-start | bytes 3145732 | tf_op jit(solution)/shard_map/cond
  229.3 8.3 %collective-permute-start.4 = (bf16[4,40,768]{2,1,0:T(8,128)(2,1)S(1)}, bf16[4,40,768]{2,1,0:T(8,128)(2,1)S(1)}, u32[]{:S(2)}, u32[]{:S(2)}) collective-permute-start(bf16[4,40,768]{2,1,0:T(8,128)(2,1)S(1)} %dynamic-slice_bitcast_fusion.1), channel_id=1, source_target_pairs={{0,2},{1,3},{2,0},{3,1},{4,6},{5,7},{6,4},{7,5},{8,10},{9,11},{10,... | collective-permute-start | bytes 737288 | tf_op jit(solution)/shard_map/cond/branch_1_fun/ppermute | solution.py:951
  231.2 17.9 %collective-permute-start.8 = (bf16[512,512]{1,0:T(8,128)(2,1)S(1)}, bf16[512,512]{1,0:T(8,128)(2,1)S(1)}, u32[]{:S(2)}, u32[]{:S(2)}) collective-permute-start(bf16[512,512]{1,0:T(8,128)(2,1)S(1)} %convolution_convert_fusion), channel_id=1, source_target_pairs={{0,16},{16,0},{1,17},{17,1},{2,18},{18,2},{3,19},{19,3},{4,20},{20... | collective-permute-start | bytes 1572872 | tf_op jit(solution)/shard_map/cond/branch_1_fun/ppermute | solution.py:908
  237.7 5.4 %collective-permute-start.5 = (bf16[1,40,768]{2,1,0:T(8,128)(2,1)S(1)}, bf16[1,40,768]{2,1,0:T(8,128)(2,1)S(1)}, u32[]{:S(2)}, u32[]{:S(2)}) collective-permute-start(bf16[1,40,768]{2,1,0:T(8,128)(2,1)S(1)} %get-tuple-element.397), channel_id=1, source_target_pairs={{0,4},{1,5},{2,6},{3,7},{4,0},{5,1},{6,2},{7,3},{8,12},{9,13},{10,... | collective-permute-start | bytes 184328 | tf_op jit(solution)/shard_map/cond/branch_1_fun/ppermute | solution.py:951
  240.3 6.3 %collective-permute-start.7 = (bf16[1,40,768]{2,1,0:T(8,128)(2,1)S(1)}, bf16[1,40,768]{2,1,0:T(8,128)(2,1)S(1)}, u32[]{:S(2)}, u32[]{:S(2)}) collective-permute-start(bf16[1,40,768]{2,1,0:T(8,128)(2,1)S(1)} %get-tuple-element.398), channel_id=1, source_target_pairs={{0,12},{1,13},{2,14},{3,15},{4,8},{5,9},{6,10},{7,11},{8,4},{9,5},... | collective-permute-start | bytes 184328 | tf_op jit(solution)/shard_map/cond/branch_1_fun/ppermute | solution.py:951
  240.5 8.6 %collective-permute-start.6 = (bf16[1,40,768]{2,1,0:T(8,128)(2,1)S(1)}, bf16[1,40,768]{2,1,0:T(8,128)(2,1)S(1)}, u32[]{:S(2)}, u32[]{:S(2)}) collective-permute-start(bf16[1,40,768]{2,1,0:T(8,128)(2,1)S(1)} %get-tuple-element.399), channel_id=1, source_target_pairs={{0,8},{1,9},{2,10},{3,11},{4,12},{5,13},{6,14},{7,15},{8,0},{9,1},... | collective-permute-start | bytes 184328 | tf_op jit(solution)/shard_map/cond/branch_1_fun/ppermute | solution.py:951
  250.0 4.6 %collective-permute-start.11 = (bf16[1,40,768]{2,1,0:T(8,128)(2,1)S(1)}, bf16[1,40,768]{2,1,0:T(8,128)(2,1)S(1)}, u32[]{:S(2)}, u32[]{:S(2)}) collective-permute-start(bf16[1,40,768]{2,1,0:T(8,128)(2,1)S(1)} %add_convert_fusion), channel_id=1, source_target_pairs={{0,4},{1,5},{2,6},{3,7},{4,0},{5,1},{6,2},{7,3},{8,12},{9,13},{10,... | collective-permute-start | bytes 184328 | tf_op jit(solution)/shard_map/cond/branch_1_fun/ppermute | solution.py:951
  251.0 7.3 %collective-permute-start.10 = (bf16[1,40,768]{2,1,0:T(8,128)(2,1)S(1)}, bf16[1,40,768]{2,1,0:T(8,128)(2,1)S(1)}, u32[]{:S(2)}, u32[]{:S(2)}) collective-permute-start(bf16[1,40,768]{2,1,0:T(8,128)(2,1)S(1)} %add_convert_fusion), channel_id=1, source_target_pairs={{0,8},{1,9},{2,10},{3,11},{4,12},{5,13},{6,14},{7,15},{8,0},{9,1},... | collective-permute-start | bytes 184328 | tf_op jit(solution)/shard_map/cond/branch_1_fun/ppermute | solution.py:951
  252.0 6.9 %collective-permute-start.9 = (bf16[1,40,768]{2,1,0:T(8,128)(2,1)S(1)}, bf16[1,40,768]{2,1,0:T(8,128)(2,1)}, u32[]{:S(2)}, u32[]{:S(2)}) collective-permute-start(bf16[1,40,768]{2,1,0:T(8,128)(2,1)S(1)} %add_convert_fusion), channel_id=1, source_target_pairs={{0,12},{1,13},{2,14},{3,15},{4,8},{5,9},{6,10},{7,11},{8,4},{9,5},... | collective-permute-start | bytes 184328 | tf_op jit(solution)/shard_map/cond/branch_1_fun/ppermute | solution.py:951
  260.5 12.3 %collective-permute-start.14 = (bf16[4,40,768]{2,1,0:T(8,128)(2,1)}, bf16[4,40,768]{2,1,0:T(8,128)(2,1)}, u32[]{:S(2)}, u32[]{:S(2)}) collective-permute-start(bf16[4,40,768]{2,1,0:T(8,128)(2,1)} %maximum_bitcast_fusion), channel_id=1, source_target_pairs={{0,2},{1,3},{2,0},{3,1},{4,6},{5,7},{6,4},{7,5},{8,10},{9,11},{10,... | collective-permute-start | bytes 737288 | tf_op jit(solution)/shard_map/cond/branch_1_fun/ppermute | solution.py:951
  261.1 12.7 %collective-permute-start.13 = (bf16[4,40,768]{2,1,0:T(8,128)(2,1)}, bf16[4,40,768]{2,1,0:T(8,128)(2,1)}, u32[]{:S(2)}, u32[]{:S(2)}) collective-permute-start(bf16[4,40,768]{2,1,0:T(8,128)(2,1)} %maximum_bitcast_fusion), channel_id=1, source_target_pairs={{0,16},{1,17},{2,18},{3,19},{4,20},{5,21},{6,22},{7,23},{8,24},{9,... | collective-permute-start | bytes 737288 | tf_op jit(solution)/shard_map/cond/branch_1_fun/ppermute | solution.py:951
  262.0 14.0 %collective-permute-start.12 = (bf16[4,40,768]{2,1,0:T(8,128)(2,1)}, bf16[4,40,768]{2,1,0:T(8,128)(2,1)}, u32[]{:S(2)}, u32[]{:S(2)}) collective-permute-start(bf16[4,40,768]{2,1,0:T(8,128)(2,1)} %maximum_bitcast_fusion), channel_id=1, source_target_pairs={{0,18},{1,19},{2,16},{3,17},{4,22},{5,23},{6,20},{7,21},{8,26},{9,... | collective-permute-start | bytes 737288 | tf_op jit(solution)/shard_map/cond/branch_1_fun/ppermute | solution.py:951
  278.2 2.9 collective-permute-start.15
  289.3 34.9 %copy-start.27 = (f32[512]{0:T(512)}, f32[512]{0:T(512)S(1)}, u32[]{:S(2)}) copy-start(f32[512]{0:T(512)S(1)} %get-tuple-element.363) | copy-start | bytes 6148
  289.3 34.9 %copy-start.28 = (f32[512]{0:T(512)}, f32[512]{0:T(512)S(1)}, u32[]{:S(2)}) copy-start(f32[512]{0:T(512)S(1)} %get-tuple-element.362) | copy-start | bytes 6148
  315.9 2.3 copy-start
  (7 other events, 6.0 us)
Sparse Core Ops, SparseCore 0:
  156.7 157.2 all-reduce.1
